TPU v7x, 32 devices: a whole 2x2x4 slice. The times are simulated.
32 devices in a mesh: ctx: 8 (over z, x), head: 4 (over y, core).
Axes of the slice: x: 2, y: 2, z: 4, core: 2. Of those that a mesh axis runs over, the one named last changes fastest.
Arguments:
- signal: bfloat16 [8192, 8192], P('ctx', 'head'), may hold values from -6 to 6
- step_size: float32 [128, 8192], P('head', 'ctx'), may hold values from 0.005 to 0.05
- log_decay: float32 [128, 8192], P('head', 'ctx'), may hold values from -0.7 to 0, as said below
- input_map: bfloat16 [8192, 1024], P('ctx', 'head'), may hold values from -1.75 to 1.75
- output_map: bfloat16 [8192, 1024], P('ctx', 'head'), may hold values from -1.75 to 1.75
- skip_gain: float32 [128], P('head'), may hold values from 0.5 to 2
- grad_out: bfloat16 [8192, 8192], P('ctx', 'head'), may hold values from -18 to 18
Outputs:
- grad_signal: bfloat16 [8192, 8192], P('ctx', 'head')
- grad_step: float32 [128, 8192], P('head', 'ctx')
- grad_decay: float32 [128, 8192], P('head', 'ctx')
- grad_input_map: bfloat16 [8192, 1024], P('ctx', 'head')
- grad_output_map: bfloat16 [8192, 1024], P('ctx', 'head')
- grad_skip: float32 [128], P('head')
Inputs may be any that keep to these rules, and one draw needn't show every extreme that they name: `log_decay`: log-decays of the state, never positive.
All inputs are finite; a program needn't handle non-finite values.
Results may differ from a plain program's by a relative error of at most 0.001.
Values sent between devices are 32-bit elements; how exact they have to be, the bound alone decides.
A program may use at most 192 MiB of HBM per device.

v0:
```python
import jax
import jax.numpy as jnp
from jax import lax
from jax.sharding import PartitionSpec as P

P_SIZE = 64
N = 128
BLOCK = 256


HIGH = lax.Precision.HIGHEST


def carried_in(part, axis, combine, identity, reverse):
    count = lax.axis_size(axis)
    place = lax.axis_index(axis)
    ahead = count - 1 - place if reverse else place
    gathered = jax.tree.map(lambda a: lax.all_gather(a, axis), part)
    state = jax.tree.map(lambda a, e: jnp.zeros_like(a) + jnp.asarray(e, a.dtype), part, identity)

    def one(lap, state):
        source = count - 1 - lap if reverse else lap
        return combine(
            state, jax.tree.map(lambda a: lax.dynamic_index_in_dim(a, source, 0, False), gathered)
        )

    return lax.fori_loop(0, ahead, one, state)


def block_forward(tokens_in, steps_in, decays_in, keys_in, queries_in, gains_in, block):
    length, groups, heads, width = tokens_in.shape
    entries = keys_in.shape[2]
    number = length // block
    tokens = tokens_in.reshape(number, block, groups, heads, width)
    keys = keys_in.reshape(number, block, groups, entries)
    queries = queries_in.reshape(number, block, groups, entries)
    steps = steps_in.reshape(groups, heads, number, block)
    cumulative = jnp.cumsum(decays_in.reshape(groups, heads, number, block), axis=-1)
    row_ids = lax.broadcasted_iota(jnp.int32, (block, block), 0)
    col_ids = lax.broadcasted_iota(jnp.int32, (block, block), 1)
    lower_mask = row_ids >= col_ids
    spread = cumulative[..., :, None] - cumulative[..., None, :]
    decays = jnp.exp(jnp.where(lower_mask, spread, -jnp.inf))
    scores = jnp.einsum("kqgn,ksgn->gkqs", queries, keys, precision=HIGH)
    weights = decays * scores[:, None] * steps[..., None, :]
    inner = jnp.einsum("ghkqs,ksghp->kqghp", weights, tokens, precision=HIGH)
    tails = jnp.exp(cumulative[..., -1:] - cumulative) * steps
    scaled = tokens * jnp.transpose(tails, (2, 3, 0, 1))[..., None]
    states = jnp.einsum("ksghp,ksgn->kghpn", scaled, keys, precision=HIGH)
    totals = jnp.moveaxis(cumulative[..., -1], -1, 0)

    def advance(carried, item):
        state_now, total_now = item
        return (jnp.exp(total_now)[..., None, None] * carried + state_now, carried)

    zero_state = jnp.zeros((groups, heads, width, entries), jnp.float32)
    final, entering = lax.scan(advance, zero_state, (states, totals))
    outer = jnp.einsum("kqgn,kghpn->kqghp", queries, entering, precision=HIGH)
    outer = outer * jnp.transpose(jnp.exp(cumulative), (2, 3, 0, 1))[..., None]
    result = inner + outer + gains_in[:, :, None] * tokens
    return (result.reshape(length, groups, heads, width), final)


def chain_part(decays_in, queries_in, entering):
    cumulative = jnp.cumsum(decays_in, axis=-1)
    exposure = jnp.transpose(jnp.exp(cumulative), (2, 0, 1))[..., None]
    result = jnp.einsum("tgn,ghpn->tghp", queries_in, entering, precision=HIGH) * exposure
    final = jnp.exp(cumulative[..., -1])[..., None, None] * entering
    return (result, final)


def state_only(tokens_in, steps_in, decays_in, keys_in):
    cumulative = jnp.cumsum(decays_in, axis=-1)
    tails = jnp.exp(cumulative[..., -1:] - cumulative) * steps_in
    scaled = tokens_in * jnp.transpose(tails, (2, 0, 1))[..., None]
    return jnp.einsum("tghp,tgn->ghpn", scaled, keys_in, precision=HIGH)


def join(earlier, later):
    return (earlier[0] + later[0], jnp.exp(later[0])[..., None, None] * earlier[1] + later[1])


def on_device(signal, step_size, log_decay, input_map, output_map, skip_gain, grad_out):
    heads_local = step_size.shape[0]
    length = signal.shape[0]
    groups_local = input_map.shape[1] // N
    per_group = heads_local // groups_local
    tokens = signal.astype(jnp.float32).reshape(length, groups_local, per_group, P_SIZE)
    upstream = grad_out.astype(jnp.float32).reshape(length, groups_local, per_group, P_SIZE)
    steps = step_size.reshape(groups_local, per_group, length)
    decays = log_decay.reshape(groups_local, per_group, length)
    keys = input_map.astype(jnp.float32).reshape(length, groups_local, N)
    queries = output_map.astype(jnp.float32).reshape(length, groups_local, N)
    gains = skip_gain.reshape(groups_local, per_group)
    cumulative = jnp.cumsum(decays, axis=-1)
    totals = cumulative[..., -1]
    own_state = state_only(tokens, steps, decays, keys)
    exposure = jnp.transpose(jnp.exp(cumulative), (2, 0, 1))[..., None]
    own_pull = jnp.einsum("tghp,tgn->ghpn", upstream * exposure, queries, precision=HIGH)
    zero_state = jnp.zeros_like(own_state)
    identity = (jnp.zeros_like(totals), zero_state)
    entering = carried_in((totals, own_state), "ctx", join, identity, False)[1]
    carried_grad = carried_in((totals, own_pull), "ctx", join, identity, True)[1]

    def whole(tok_in, step_in, decay_in, key_in, query_in, gain_in):
        local_out, local_end = block_forward(
            tok_in, step_in, decay_in, key_in, query_in, gain_in, BLOCK
        )
        chain_out, chain_end = chain_part(decay_in, query_in, entering)
        return (local_out + chain_out, local_end + chain_end)

    whole_value, whole_pull = jax.vjp(whole, tokens, steps, decays, keys, queries, gains)
    grads = whole_pull((upstream, carried_grad))
    grad_tokens, grad_steps, grad_decays, grad_keys, grad_queries, grad_gains = grads
    gain_total = lax.psum(grad_gains, "ctx")
    grad_signal = grad_tokens.reshape(length, heads_local * P_SIZE).astype(jnp.bfloat16)
    grad_step = grad_steps.reshape(heads_local, length)
    grad_decay = grad_decays.reshape(heads_local, length)
    grad_input_map = grad_keys.reshape(length, groups_local * N).astype(jnp.bfloat16)
    grad_output_map = grad_queries.reshape(length, groups_local * N).astype(jnp.bfloat16)
    grad_skip = gain_total.reshape(heads_local)
    return (grad_signal, grad_step, grad_decay, grad_input_map, grad_output_map, grad_skip)


def solution(mesh):
    placed = (
        P("ctx", "head"),
        P("head", "ctx"),
        P("head", "ctx"),
        P("ctx", "head"),
        P("ctx", "head"),
        P("head"),
        P("ctx", "head"),
    )
    return jax.shard_map(
        on_device,
        mesh=mesh,
        in_specs=placed,
        out_specs=(
            P("ctx", "head"),
            P("head", "ctx"),
            P("head", "ctx"),
            P("ctx", "head"),
            P("ctx", "head"),
            P("head"),
        ),
        check_vma=False,
    )
```

profile of v0, /device:TPU:0, one launch (start us, length us, event | category | flops | bytes accessed | tf_op | source)
XLA Modules:
  0.0 532.7 jit_solution(16119554467747439446)
XLA Ops:
  8.1 9.0 %reduce-window.26 = f32[2,16,8,128]{3,2,1,0:T(8,128)S(1)} reduce-window(f32[2,16,8,128]{3,2,1,0:T(8,128)S(1)} %bitcast.274, f32[]{:T(128)} %constant.141.clone.1), window={size=1x1x1x128 pad=0_0x0_0x0_0x127_0}, to_apply=%region_0.0 | reduce-window | flops 4161536 | bytes 262148 | tf_op jit(solution)/shard_map/reduce-window
  60.6 7.9 %reshape_reshape.26 = bf16[4,256,2,16,64]{1,0,4,3,2:T(4,128)(2,1)} reshape(bf16[1024,2048]{0,1:T(8,128)(2,1)} %copy.448) | data formatting | bytes 8388608 | tf_op jit(solution)/shard_map/transpose(jvp())/reshape;reshape | solution.py:61
  68.5 9.0 %reshape_reshape.23 = f32[4,256,2,16,64]{1,0,4,3,2:T(4,128)} reshape(bf16[1024,2048]{0,1:T(8,128)(2,1)} %copy.462) | data formatting | bytes 12582912 | tf_op jit(solution)/shard_map/jvp()/reshape;reshape | solution.py:34
  77.5 8.9 %reshape_reshape.21 = f32[4,256,2,16,64]{1,0,4,3,2:T(4,128)} reshape(bf16[1024,2048]{0,1:T(8,128)(2,1)} %copy.448) | data formatting | bytes 12582912 | tf_op jit(solution)/shard_map/transpose(jvp())/reshape;reshape | solution.py:61
  86.3 13.0 %reshape.233 = bf16[4,256,2,16,64]{4,3,2,1,0:T(8,128)(2,1)} reshape(bf16[1024,2048]{1,0:T(8,128)(2,1)} %param.15) | data formatting | bytes 8388608 | tf_op jit(solution)/shard_map/jvp()/reshape;reshape | solution.py:34
  110.1 24.4 %psum.7 = f32[32]{0:T(128)} all-reduce(f32[32]{0:T(128)S(1)} %reshape.218), channel_id=1, replica_groups=mesh['ctx'=8,'head'=4] {'ctx'}, use_global_device_ids=true, to_apply=%region_28.29 | all-reduce | flops 32 | bytes 256 | tf_op jit(solution)/shard_map/psum | solution.py:115
  134.5 16.9 %all-gather = f32[16,16,1]{1,2,0:T(1,128)S(1)} all-gather(f32[2,16,1]{1,2,0:T(1,128)S(1)} %bitcast.284), channel_id=2, replica_groups=mesh['ctx'=8,'head'=4] {'ctx'}, dimensions={0}, use_global_device_ids=true | all-gather | bytes 1152 | tf_op jit(solution)/shard_map/all_gather | solution.py:18
  153.8 9.3 %multiply_bitcast_fusion = f32[4,2,16,64,256]{4,0,3,2,1:T(4,128)} fusion(f32[4,256,2,16,64]{1,0,4,3,2:T(4,128)} %reshape_reshape.21, f32[4,256,2,16]{1,0,3,2:T(4,128)S(1)} %copy.459), kind=kLoop, calls=%fused_computation.53 | loop fusion | flops 2097152 | bytes 16908288 | tf_op jit(solution)/shard_map/transpose(jvp(kqgn,kghpn->kqghp))/transpose | solution.py:58
  163.2 10.0 %fusion.29 = f32[4,2,16,64,128]{4,3,2,1,0:T(8,128)} fusion(f32[4,2,16,64,256]{4,0,3,2,1:T(4,128)} %multiply_bitcast_fusion, bf16[4,256,2,128,1]{3,2,1,0,4:T(2,128)(2,1)S(1)} %bitcast.252), kind=kOutput, calls=%fused_computation.57 | convolution fusion | flops 3221225472 | bytes 13107200 | tf_op jit(solution)/shard_map/transpose(jvp(kqgn,kghpn->kqghp))/dot_general | solution.py:58
  173.2 10.1 %fusion.35 = f32[4,2,16,64,128]{4,3,2,1,0:T(8,128)} fusion(f32[4,256,2,16,64]{1,0,4,3,2:T(4,128)} %reshape_reshape.23, f32[4,256,2,16]{1,3,2,0:T(8,128)S(1)} %get-tuple-element.549, bf16[4,256,2,128,1]{3,2,1,0,4:T(2,128)(2,1)S(1)} %bitcast.254), kind=kOutput, calls=%fused_computation.63 | convolution fusion | flops 3223322624 | bytes 13238272 | tf_op jit(solution)/shard_map/jvp(ksghp,ksgn->kghpn)/dot_general | solution.py:49
  185.9 12.4 %while.64 = (s32[]{:T(128)}, f32[2,16,64,128]{3,2,1,0:T(8,128)S(1)}, f32[4,2,16,64,128]{4,3,2,1,0:T(8,128)}, f32[4,2,16]{2,1,0:T(2,128)S(1)}, f32[4,2,16,1,1]{2,...) while((s32[]{:T(128)}, ...), condition=%wide.region_7.8_spmd.clone, body=%wide.region_6.7_spmd.clone.sunk | while | flops 1048579 | bytes 5247620 | solution.py:57
  198.3 19.1 %fusion.48 = f32[4,256,2,128]{3,1,2,0:T(8,128)} fusion(f32[4,2,16,64,128]{4,3,2,1,0:T(8,128)} %get-tuple-element.777, f32[4,2,16,64,256]{4,0,3,2,1:T(4,128)} %multiply_bitcast_fusion), kind=kOutput, calls=%fused_computation.74 | convolution fusion | flops 3221225472 | bytes 13631488 | tf_op jit(solution)/shard_map/transpose(jvp(kqgn,kghpn->kqghp))/dot_general | solution.py:58
  217.5 8.7 %fusion.18 = f32[4,256,2,16]{1,3,2,0:T(8,128)} fusion(f32[4,256,2,16,64]{1,0,4,3,2:T(4,128)} %reshape_reshape.21, f32[4,2,16,64,128]{4,3,2,1,0:T(8,128)S(1)} %copy-done.1, bf16[4,256,2,128,1]{3,2,1,0,4:T(2,128)(2,1)S(1)} %bitcast.253), kind=kOutput, calls=%fused_computation.39 | convolution fusion | flops 3225387008 | bytes 13238272 | tf_op jit(solution)/shard_map/jvp(kqgn,kghpn->kqghp)/dot_general | solution.py:58
  233.0 61.6 %all-gather.6.cloned.1.call-done = f32[16,16,64,128]{3,2,1,0:T(8,128)} async-done(((f32[2,16,64,128]{3,2,1,0:T(8,128)}), f32[16,16,64,128]{3,2,1,0:T(8,128)}) %all-gather.6.cloned.1.call-update) | async-done | bytes 8388624 | tf_op jit(solution)/shard_map/all_gather | solution.py:18
  294.8 15.1 %while.61 = (s32[]{:T(128)}, f32[2,16,64,128]{3,2,1,0:T(8,128)S(1)}, s32[]{:T(128)}, f32[8,2,16]{2,1,0:T(2,128)}, f32[8,2,16,64,128]{4,3,2,1,0:T(8,128)}, /*index=5*/s32[]{:T(128)}, s32[]{:T(128)}, s32[]{:T(128)}, s32[]{:T(128)}) while((s32[]{:T(128)}, f32[2,16,64,128]{3,2,1,0:T(8,128)S(1)}, s32[]{:T(128)}, f32[8,2,16]{2,1,0:T(2,128)}, ...), condition=%wide.region_3.4_spmd, body=%wide.region_2.3_spmd.sunk | while | flops 524294 | bytes 3146267 | solution.py:27
  313.8 17.4 %while.62 = (s32[]{:T(128)}, f32[2,16,64,128]{3,2,1,0:T(8,128)S(1)}, f32[4,2,16,64,128]{4,3,2,1,0:T(8,128)}, f32[4,2,16]{2,1,0:T(2,128)}, f32[4,2,16,64,128]{4,3...) while((s32[]{:T(128)}, ...), condition=%wide.region_10.11_spmd, body=%wide.region_8.10_spmd.sunk | while | flops 1048579 | bytes 6293377 | solution.py:57
  331.2 13.6 %fusion.47 = f32[4,256,2,128]{1,3,2,0:T(8,128)} fusion(f32[4,2,16,64,128]{4,3,2,1,0:T(8,128)} %get-tuple-element.338, f32[4,256,2,16,64]{1,0,4,3,2:T(4,128)} %reshape_reshape.23, f32[4,256,2,16]{1,3,2,0:T(8,128)S(1)} %get-tuple-element.549), kind=kOutput, calls=%fused_computation.73 | convolution fusion | flops 3223322624 | bytes 13762560 | tf_op jit(solution)/shard_map/transpose(jvp(ksghp,ksgn->kghpn))/dot_general | solution.py:49
  344.8 10.7 %fusion.24 = (f32[4,256,2,16]{1,3,2,0:T(8,128)}, f32[4,2,16,64,256]{4,3,2,1,0:T(8,128)}) fusion(f32[4,256,2,16,64]{1,0,4,3,2:T(4,128)} %reshape_reshape.23, f32[4,2,16,64,128]{4,3,2,1,0:T(8,128)S(1)} %copy-done.2, bf16[4,256,2,128,1]{3,2,1,0,4:T(2,128)(2,1)S(1)} %bitcast.255), kind=kOutput, calls=%fused_computation.49 | convolution fusion | flops 3225387008 | bytes 21626880 | tf_op jit(solution)/shard_map/transpose(jvp(ksghp,ksgn->kghpn))/dot_general | solution.py:49
  362.7 39.6 %reduce-window.34 = f32[2,16,8,128]{3,2,1,0:T(8,128)S(1)} reduce-window(f32[2,16,8,128]{3,2,1,0:T(8,128)S(1)} %copy.489, f32[]{:T(128)} %constant.141.clone.1), window={size=1x1x1x128 pad=0_0x0_0x0_0x0_127}, to_apply=%region_17.18 | reduce-window | flops 4161536 | bytes 262148 | tf_op jit(solution)/shard_map/reduce-window.4
  406.0 26.4 %fusion.22 = bf16[4,256,2,16,64]{1,4,3,2,0:T(8,128)(2,1)} fusion(f32[4,2,16,64,256]{4,3,2,1,0:T(8,128)} %get-tuple-element.552, f32[4,256,2,16,64]{1,0,4,3,2:T(4,128)} %reshape_reshape.21, f32[4,256,2,16]{1,3,2,0:T(8,128)S(1)} %get-tuple-element.549, f32[2,16]{1,0:T(2,128)} %mul.216, bf16[4,2,16,64,256]{4,0,3,2,1:T(4,128)(2,1)} %bitcast.260, ...), kind=kOutput, calls=%fused_computation.45 | convolution fusion | flops 6486491136 | bytes 27721856 | tf_op jit(solution)/shard_map/transpose(jvp(ghkqs,ksghp->kqghp))/dot_general | solution.py:46
  432.4 12.9 %copy.535 = bf16[4,256,2,16,64]{4,3,2,1,0:T(8,128)(2,1)} copy(bf16[4,256,2,16,64]{1,4,3,2,0:T(8,128)(2,1)} %fusion.22) | data formatting | bytes 8388608
  445.3 12.4 %reshape.232 = bf16[1024,2048]{1,0:T(8,128)(2,1)} reshape(bf16[4,256,2,16,64]{4,3,2,1,0:T(8,128)(2,1)} %copy.535) | data formatting | bytes 8388608
  457.7 27.6 %fusion.9 = (f32[2,16,4,256]{3,1,0,2:T(8,128)}, f32[2,16,4,256]{3,1,0,2:T(8,128)}, f32[2,16,4,256]{3,1,0,2:T(8,128)}, f32[2,4,256,256]{3,2,0,1:T(8,128)S(1)}) fusion(f32[2,16,4,256]{3,1,0,2:T(8,128)} %copy-done.17, f32[2,4,256,256]{3,2,0,1:T(8,128)} %fusion.66, f32[2,16,4,256]{3,1,0,2:T(8,128)S(1)} %copy-done.16, pred[256,256]{1,0:T(8,128)(4,1)} %iota_compare_fusion, ...), kind=kOutput, calls=%fused_computation.29 | convolution fusion | flops 1182171136 | bytes 13303808 | tf_op jit(solution)/shard_map/transpose(jvp(ghkqs,ksghp->kqghp))/dot_general | solution.py:46
  502.9 19.9 %reduce-window.36 = f32[2,16,4,2,128]{4,1,2,3,0:T(8,128)S(1)} reduce-window(f32[2,16,4,2,128]{4,1,2,3,0:T(8,128)S(1)} %copy.499, f32[]{:T(128)} %constant.141.clone.1), window={size=1x1x1x1x128 pad=0_0x0_0x0_0x0_0x0_127}, to_apply=%region_23.24 | reduce-window | flops 4161536 | bytes 262148 | tf_op jit(solution)/shard_map/reduce-window.6
  (184 shorter events, 146.4 us)
Async XLA Ops:
  7.2 219.0 %all-gather.8.cloned.1.call-start = ((), (), s32[]{:S(2)}) async-start(), calls=%async_computation.1 | async-start | bytes 9437184 | tf_op jit(solution)/shard_map/all_gather | solution.py:18
  19.3 16.5 %copy-start.3 = (f32[2,16,8,128]{1,0,3,2:T(2,128)}, f32[2,16,8,128]{1,0,3,2:T(2,128)S(1)}, u32[]{:S(2)}) copy-start(f32[2,16,8,128]{1,0,3,2:T(2,128)S(1)} %copy.452) | copy-start | bytes 393220
  35.8 5.3 copy-start.8
  40.8 253.8 %all-gather.6.cloned.1.call-start = ((), (), s32[]{:S(2)}) async-start(), calls=%async_computation | async-start | bytes 9437184 | tf_op jit(solution)/shard_map/all_gather | solution.py:18
  41.6 9.8 %copy-start.11 = (f32[1024,2,16]{0,2,1:T(8,128)}, f32[1024,2,16]{0,2,1:T(8,128)S(1)}, u32[]{:S(2)}) copy-start(f32[1024,2,16]{0,2,1:T(8,128)S(1)} %copy.454) | copy-start | bytes 393220
  51.4 3.6 copy-start
  51.4 8.8 %copy-start.13 = (f32[32,1024]{1,0:T(8,128)S(1)}, f32[32,1024]{1,0:T(8,128)}, u32[]{:S(2)}) copy-start(f32[32,1024]{1,0:T(8,128)} %param.16) | copy-start | bytes 393220
  51.4 8.8 %copy-start.14 = (f32[32,1024]{1,0:T(8,128)S(1)}, f32[32,1024]{1,0:T(8,128)}, u32[]{:S(2)}) copy-start(f32[32,1024]{1,0:T(8,128)} %param.17) | copy-start | bytes 393220
  51.4 8.9 %copy-start.7 = (bf16[1024,256]{1,0:T(8,128)(2,1)S(1)}, bf16[1024,256]{1,0:T(8,128)(2,1)}, u32[]{:S(2)}) copy-start(bf16[1024,256]{1,0:T(8,128)(2,1)} %param.18) | copy-start | bytes 1572868
  51.4 9.1 %copy-start.9 = (bf16[1024,256]{1,0:T(8,128)(2,1)S(1)}, bf16[1024,256]{1,0:T(8,128)(2,1)}, u32[]{:S(2)}) copy-start(bf16[1024,256]{1,0:T(8,128)(2,1)} %param.19) | copy-start | bytes 1572868
  86.3 13.0 %copy-start.21 = (f32[32]{0:T(128)S(1)}, f32[32]{0:T(128)}, u32[]{:S(2)}) copy-start(f32[32]{0:T(128)} %param.20) | copy-start | bytes 388
  198.3 19.1 %copy-start.1 = (f32[4,2,16,64,128]{4,3,2,1,0:T(8,128)S(1)}, f32[4,2,16,64,128]{4,3,2,1,0:T(8,128)}, u32[]{:S(2)}) copy-start(f32[4,2,16,64,128]{4,3,2,1,0:T(8,128)} %get-tuple-element.777) | copy-start | bytes 12582916
  226.3 68.4 %copy-start.18 = (f32[8,2,16]{2,1,0:T(2,128)}, f32[8,2,16]{2,1,0:T(2,128)S(1)}, u32[]{:S(2)}) copy-start(f32[8,2,16]{2,1,0:T(2,128)S(1)} %get-tuple-element.833) | copy-start | bytes 3076
  331.2 13.6 %copy-start.2 = (f32[4,2,16,64,128]{4,3,2,1,0:T(8,128)S(1)}, f32[4,2,16,64,128]{4,3,2,1,0:T(8,128)}, u32[]{:S(2)}) copy-start(f32[4,2,16,64,128]{4,3,2,1,0:T(8,128)} %get-tuple-element.338) | copy-start | bytes 12582916
  344.8 10.7 %copy-start.4 = (f32[2,16,8,128]{1,0,3,2:T(2,128)S(1)}, f32[2,16,8,128]{1,0,3,2:T(2,128)}, u32[]{:S(2)}) copy-start(f32[2,16,8,128]{1,0,3,2:T(2,128)} %copy-done.3) | copy-start | bytes 393220
  344.8 10.7 %copy-start.20 = (f32[2,16]{1,0:T(2,128)S(1)}, f32[2,16]{1,0:T(2,128)}, u32[]{:S(2)}) copy-start(f32[2,16]{1,0:T(2,128)} %multiply_reduce_fusion.2) | copy-start | bytes 388
  344.8 58.6 %copy-start.19 = (f32[4,2,16]{2,1,0:T(2,128)S(1)}, f32[4,2,16]{2,1,0:T(2,128)}, u32[]{:S(2)}) copy-start(f32[4,2,16]{2,1,0:T(2,128)} %get-tuple-element.340) | copy-start | bytes 1540
  405.2 27.1 %copy-start.15 = (f32[2,16,4,256]{3,1,0,2:T(8,128)}, f32[2,16,4,256]{3,1,0,2:T(8,128)S(1)}, u32[]{:S(2)}) copy-start(f32[2,16,4,256]{3,1,0,2:T(8,128)S(1)} %get-tuple-element.547) | copy-start | bytes 393220
  405.2 27.1 %copy-start.17 = (f32[2,16,4,256]{3,1,0,2:T(8,128)}, f32[2,16,4,256]{3,1,0,2:T(8,128)S(1)}, u32[]{:S(2)}) copy-start(f32[2,16,4,256]{3,1,0,2:T(8,128)S(1)} %get-tuple-element.548) | copy-start | bytes 393220
  445.3 12.4 %copy-start.16 = (f32[2,16,4,256]{3,1,0,2:T(8,128)S(1)}, f32[2,16,4,256]{3,1,0,2:T(8,128)}, u32[]{:S(2)}) copy-start(f32[2,16,4,256]{3,1,0,2:T(8,128)} %copy-done.15) | copy-start | bytes 393220
  457.6 27.6 %copy-start.6 = (f32[4,256,2,128]{1,3,2,0:T(8,128)S(1)}, f32[4,256,2,128]{1,3,2,0:T(8,128)}, u32[]{:S(2)}) copy-start(f32[4,256,2,128]{1,3,2,0:T(8,128)} %fusion.47) | copy-start | bytes 3145732
  457.7 29.4 %copy-start.5 = (f32[4,256,2,128]{3,1,2,0:T(8,128)S(1)}, f32[4,256,2,128]{3,1,2,0:T(8,128)}, u32[]{:S(2)}) copy-start(f32[4,256,2,128]{3,1,2,0:T(8,128)} %fusion.48) | copy-start | bytes 3145732
  485.2 6.2 %copy-start.12 = (f32[1024,2,16]{0,2,1:T(8,128)S(1)}, f32[1024,2,16]{0,2,1:T(8,128)}, u32[]{:S(2)}) copy-start(f32[1024,2,16]{0,2,1:T(8,128)} %copy-done.11) | copy-start | bytes 393220
  491.4 8.8 %copy-start.10 = (bf16[4,256,2,128]{1,3,2,0:T(8,128)(2,1)S(1)}, bf16[4,256,2,128]{1,3,2,0:T(8,128)(2,1)}, u32[]{:S(2)}) copy-start(bf16[4,256,2,128]{1,3,2,0:T(8,128)(2,1)} %fusion.62) | copy-start | bytes 1572868
Sparse Core Ops, SparseCore 0:
  41.0 128.3 all-gather.7
  171.5 123.1 all-gather.5
where the time goes:
time: 541 us; the launch traced here: 533 us
  matrix products  156 us (29%)
  other arithmetic  137 us (25%)
  local copies, waits for them, and re-layouts  120 us (22%)
  waiting for transfers between devices  61.7 us (11%)
  blocking collectives  41.3 us (8%)
  between operations  14.8 us (3%)
    another operation x12, other arithmetic  74.2 us
    all_gather x2, waiting for transfers between devices, carried_in(): gathered = jax.tree.map(lambda a: lax.all_gather(a, axis), part)  61.6 us
    dot_general x2, matrix products, block_forward(): inner = jnp.einsum('ghkqs,ksghp->kqghp', weights, tokens, precision=HIGH)  53.9 us
    unnamed x52, local copies, waits for them, and re-layouts  45.3 us
    dot_general x3, matrix products, block_forward(): outer = jnp.einsum('kqgn,kghpn->kqghp', queries, entering, precision=HIGH)  37.8 us
    dot_general x3, matrix products, block_forward(): states = jnp.einsum('ksghp,ksgn->kghpn', scaled, keys, precision=HIGH)  34.3 us
    psum x1, blocking collectives, on_device(): gain_total = lax.psum(grad_gains, 'ctx')  24.4 us
    another operation x2, local copies, waits for them, and re-layouts, block_forward(): tokens = tokens_in.reshape(number, block, groups, heads, width)  21.9 us
  transfers between devices with their start and end apart: 2, of which 1 were waited for; matrix products, arithmetic and copies ran while one was open for 28% of the time, Pallas kernels for 0%

commit v1 on v0

v1 whole, which is shorter than its diff:
```python
import functools

import jax
import jax.numpy as jnp
from jax import lax
from jax.experimental import pallas as pl
from jax.experimental.pallas import tpu as pltpu
from jax.sharding import PartitionSpec as P

P_SIZE = 64
N = 128
C = 128
LOG2E = 1.4426950408889634
F32 = jnp.float32
BF16 = jnp.bfloat16
NT = (((1,), (1,)), ((), ()))
TN = (((0,), (0,)), ((), ()))
NN = (((1,), (0,)), ((), ()))


def dot(a, b, dims):
    return lax.dot_general(a, b, dims, preferred_element_type=F32)


def split(a):
    high = a.astype(BF16)
    return high, (a - high.astype(F32)).astype(BF16)


def halves():
    lane = lax.broadcasted_iota(jnp.int32, (1, 2 * P_SIZE), 1)
    low = (lane < P_SIZE).astype(F32)
    return low, 1.0 - low


def blocks_of(pair):
    low, high = halves()
    return jnp.concatenate([pair * low.astype(pair.dtype), pair * high.astype(pair.dtype)], axis=0)


def params(**more):
    return pltpu.CompilerParams(vmem_limit_bytes=48 * 1024 * 1024, **more)


def prep_kernel(groups, per, decay_ref, step_ref, col_ref, row_ref):
    heads = decay_ref.shape[0]
    lane = lax.broadcasted_iota(jnp.int32, (heads, C), 1)
    for k in range(decay_ref.shape[1] // C):
        at = slice(k * C, (k + 1) * C)
        step = step_ref[:, at]
        cum = decay_ref[:, at]
        shift = 1
        while shift < C:
            cum = cum + jnp.where(lane >= shift, pltpu.roll(cum, shift, 1), 0.0)
            shift *= 2
        total = cum[:, C - 1 :]
        cum2 = cum * LOG2E
        row_ref[:, at] = cum2 - jnp.log(step) * LOG2E
        rise = jnp.exp(cum)
        tail = jnp.exp(total - cum) * step
        for g in range(groups):
            own = slice(g * per, (g + 1) * per)
            pad = jnp.zeros((C - 3 * per, C), F32)
            stacked = jnp.concatenate([cum2[own], rise[own], tail[own], pad], axis=0)
            col_ref[at, g * C : (g + 1) * C] = stacked.T


def state_kernel(per, x_ref, dy_ref, k_ref, q_ref, colx_ref, coly_ref, ex_ref, ey_ref,
                 h_ref, g_ref, ends_ref, h_s, g_s):
    k = pl.program_id(1)

    @pl.when(k == 0)
    def _():
        h_s[...] = jnp.zeros_like(h_s)
        g_s[...] = jnp.zeros_like(g_s)

    low, _ = halves()
    keys = jnp.concatenate([k_ref[...]] * 2, axis=0)
    queries = jnp.concatenate([q_ref[...]] * 2, axis=0)
    colx = colx_ref[...]
    coly = coly_ref[...]

    def scaled(ref, col, first):
        parts = []
        for j in range(per // 2):
            a = first + 2 * j
            factor = jnp.where(low > 0, col[:, a : a + 1], col[:, a + 1 : a + 2])
            parts.append(ref[:, 128 * j : 128 * (j + 1)].astype(F32) * factor)
        return jnp.concatenate(split(jnp.concatenate(parts, axis=1)), axis=0)

    h_ref[0] = h_s[...]
    g_ref[0] = g_s[...]
    h_s[...] = ex_ref[0] * h_s[...] + dot(keys, scaled(x_ref, colx, 2 * per), TN)
    g_s[...] = ey_ref[0] * g_s[...] + dot(queries, scaled(dy_ref, coly, per), TN)

    @pl.when(k == pl.num_programs(1) - 1)
    def _():
        ends_ref[0] = h_s[...]
        ends_ref[1] = g_s[...]


def inner_kernel(per, carried, x_ref, dy_ref, k_ref, q_ref, col_ref, row_ref, *rest):
    z_ref, gq_ref, gk_ref, r_ref, skip_ref = rest[carried:]
    lane = lax.broadcasted_iota(jnp.int32, (C, C), 1)
    mask = lax.broadcasted_iota(jnp.int32, (C, C), 0) >= lane
    keys = k_ref[...]
    queries = q_ref[...]
    scores = dot(queries, keys, NT)
    col = col_ref[...]
    row = row_ref[...]
    total = jnp.zeros((C, C), F32)
    sums = jnp.zeros((C, C), F32)
    for j in range(per // 2):
        at = slice(128 * j, 128 * (j + 1))
        x = x_ref[:, at]
        dy = dy_ref[:, at]
        met = dot(dy, blocks_of(x), NT)
        highs, lows = [], []
        for i in range(2):
            a = 2 * j + i
            spread = jnp.where(mask, col[:, a : a + 1] - row[a : a + 1, :], -1e4)
            decay = jnp.exp2(spread)
            lm = decay * met[:, i * C : (i + 1) * C]
            total = total + lm
            sums = jnp.where(lane == a, jnp.sum(lm * scores, axis=1, keepdims=True), sums)
            high, rest_of = split(decay * scores)
            highs.append(high)
            lows.append(rest_of)
        ups = blocks_of(dy)
        z_ref[:, at] = dot(jnp.concatenate(highs, axis=0), ups, TN) + dot(
            jnp.concatenate(lows, axis=0), ups, TN
        )
        skip_ref[0, :, at] = jnp.sum(x.astype(F32) * dy.astype(F32), axis=0, keepdims=True)
    high, rest_of = split(total)
    gq_ref[...] = dot(high, keys, NN) + dot(rest_of, keys, NN)
    gk_ref[...] = dot(high, queries, TN) + dot(rest_of, queries, TN)
    r_ref[...] = sums


def outer_kernel(per, x_ref, dy_ref, k_ref, q_ref, col_ref, step_ref, h_ref, g_ref, ends_ref,
                 pre_ref, post_ref, tot_ref, gain_ref, z_ref, gq_ref, gk_ref, r_ref,
                 gx_ref, gstep_ref, gdecay_ref, gkey_ref, gquery_ref):
    lane = lax.broadcasted_iota(jnp.int32, (C, C), 1)
    last = lax.broadcasted_iota(jnp.int32, (C, C), 0) == C - 1
    low, high_half = halves()
    keys2 = jnp.concatenate([k_ref[...]] * 2, axis=1)
    queries = q_ref[...].astype(F32)
    col = col_ref[...]
    gq = gq_ref[...]
    gk = gk_ref[...]
    pack = r_ref[...]
    for j in range(per // 2):
        at = slice(128 * j, 128 * (j + 1))
        x = x_ref[:, at]
        dy = dy_ref[:, at]
        state = h_ref[0, :, at] + pre_ref[0, :, at] * ends_ref[0, :, at]
        pull = g_ref[0, :, at] + post_ref[0, :, at] * ends_ref[1, :, at]
        s_high, s_low = split(state)
        p_high, p_low = split(pull)
        s_both = jnp.concatenate([blocks_of(s_high), blocks_of(s_low)], axis=1)
        p_both = jnp.concatenate([blocks_of(p_high), blocks_of(p_low)], axis=1)
        to_q = dot(jnp.concatenate([dy, dy], axis=1), s_both, NT)
        to_k = dot(jnp.concatenate([x, x], axis=1), p_both, NT)
        z_out = dot(keys2, jnp.concatenate([p_high, p_low], axis=0), NN)
        a = 2 * j
        tails = [col[:, 2 * per + a + i : 2 * per + a + i + 1] for i in range(2)]
        z_out = z_out * jnp.where(low > 0, tails[0], tails[1])
        z = z_ref[:, at] + z_out
        gx_ref[:, at] = (z + gain_ref[:, at] * dy.astype(F32)).astype(BF16)
        xf = x.astype(F32)
        xz = xf * z
        edge = jnp.sum(xf * z_out + tot_ref[0, :, at] * (state * pull), axis=0, keepdims=True)
        for i, half in enumerate((low, high_half)):
            rise = col[:, per + a + i : per + a + i + 1]
            own = to_q[:, i * C : (i + 1) * C] * rise
            gq = gq + own
            gk = gk + to_k[:, i * C : (i + 1) * C] * tails[i]
            rows = jnp.sum(own * queries, axis=1, keepdims=True)
            cols = jnp.sum(xz * half, axis=1, keepdims=True)
            edge_sum = jnp.sum(edge * half, axis=1, keepdims=True)
            pack = jnp.where(lane == a + i, pack + (rows - cols), pack)
            pack = jnp.where((lane == a + i) & last, pack + edge_sum, pack)
            pack = jnp.where(lane == per + a + i, cols, pack)
    gquery_ref[...] = gq.astype(BF16)
    gkey_ref[...] = gk.astype(BF16)
    turned = pack.T
    part = turned[:per]
    lane16 = lax.broadcasted_iota(jnp.int32, (per, C), 1)
    shift = 1
    while shift < C:
        part = part + jnp.where(lane16 < C - shift, pltpu.roll(part, C - shift, 1), 0.0)
        shift *= 2
    gdecay_ref[...] = part
    gstep_ref[...] = turned[per : 2 * per] / step_ref[...]


def exchange(parts, nx, x, nz):
    kept = lax.dynamic_index_in_dim(parts, x, 1, False)
    got = [kept]
    for r in range(1, nx):
        pairs = [(c * nx + i, c * nx + (i + r) % nx) for c in range(nz) for i in range(nx)]
        sent = lax.dynamic_index_in_dim(parts, (x + r) % nx, 1, False)
        got.append(lax.ppermute(sent, "ctx", pairs))
    return got


def by_sender(got, nx, x):
    out = []
    for j in range(nx):
        one = got[0]
        for r in range(1, nx):
            one = jnp.where((x - j) % nx == r, got[r], one)
        out.append(one)
    return out


def held(value, work):
    return lax.optimization_barrier((value, work))


def carry(ends, fade, stages, work):
    count = lax.axis_size("ctx")
    nx = 2 if count < 16 else 4
    nz = count // nx
    place = lax.axis_index("ctx")
    x, z = place % nx, place // nx
    turns = [[(c * nx + i, c * nx + (i + r) % nx) for c in range(nz) for i in range(nx)] for r in range(nx)]
    row_fade = by_sender([fade] + [lax.ppermute(fade, "ctx", t) for t in turns[1:]], nx, x)
    all_fade = functools.reduce(lambda a, b: a * b, row_fade)

    _, rows, width = ends.shape
    got = exchange(ends.reshape(2, nx, rows // nx, width), nx, x, nz)
    work = stages[0](work)
    got, work = held(got, work)
    both = by_sender(got, nx, x)
    states, pulls = [b[0] for b in both], [b[1] for b in both]
    state_sum = states[0]
    for i in range(1, nx):
        state_sum = row_fade[i] * state_sum + states[i]
    pull_sum = pulls[nx - 1]
    for i in range(nx - 2, -1, -1):
        pull_sum = row_fade[i] * pull_sum + pulls[i]
    entering, leaving, up_send, down_send = None, None, state_sum, pull_sum
    for hop in range(nz - 1):
        up = [(hop * nx + i, (hop + 1) * nx + i) for i in range(nx)]
        down = [((nz - 1 - hop) * nx + i, (nz - 2 - hop) * nx + i) for i in range(nx)]
        came = (lax.ppermute(up_send, "ctx", up), lax.ppermute(down_send, "ctx", down))
        work = stages[1 + hop](work)
        came, work = held(came, work)
        entering = came[0] if hop == 0 else entering + came[0]
        leaving = came[1] if hop == 0 else leaving + came[1]
        up_send = all_fade * entering + state_sum
        down_send = all_fade * leaving + pull_sum
    ins, outs = [entering], [leaving]
    for i in range(nx - 1):
        ins.append(row_fade[i] * ins[-1] + states[i])
    for i in range(nx - 1, 0, -1):
        outs.append(row_fade[i] * outs[-1] + pulls[i])
    got = exchange(jnp.stack([jnp.stack(ins), jnp.stack(outs[::-1])]), nx, x, nz)
    work = stages[nz](work)
    got, work = held(got, work)
    both = jnp.stack(by_sender(got, nx, x), axis=1)
    return both.reshape(2, rows, width), work


def on_device(signal, step_size, log_decay, input_map, output_map, skip_gain, grad_out):
    heads, length = step_size.shape
    groups = input_map.shape[1] // N
    per = heads // groups
    wide = per * P_SIZE
    width = heads * P_SIZE
    nk = length // C

    col, row = pl.pallas_call(
        functools.partial(prep_kernel, groups, per),
        out_shape=(
            jax.ShapeDtypeStruct((length, groups * C), F32),
            jax.ShapeDtypeStruct((heads, length), F32),
        ),
        compiler_params=params(),
        name="prep",
    )(log_decay, step_size)

    sums = jnp.sum(log_decay.reshape(heads, nk, C), axis=-1)
    after = lax.broadcasted_iota(jnp.int32, (nk, nk), 0) > lax.broadcasted_iota(jnp.int32, (nk, nk), 1)
    before = jnp.sum(jnp.where(after.T[None], sums[:, :, None], 0.0), axis=1)
    behind = jnp.sum(jnp.where(after[None], sums[:, :, None], 0.0), axis=1)

    def lanes(a):
        return jnp.repeat(jnp.exp(a.T), P_SIZE, axis=1)[:, None, :]

    tot, pre, post = lanes(sums), lanes(before), lanes(behind)
    gains = jnp.repeat(skip_gain, P_SIZE)[None, :]

    def spec(shape, index):
        return pl.BlockSpec(shape, index)

    big = spec((C, wide), lambda g, k: (k, g))
    big_r = spec((C, wide), lambda g, k: (nk - 1 - k, g))
    small = spec((C, C), lambda g, k: (k, g))
    small_r = spec((C, C), lambda g, k: (nk - 1 - k, g))
    line = spec((1, 1, wide), lambda g, k: (k, 0, g))
    line_r = spec((1, 1, wide), lambda g, k: (nk - 1 - k, 0, g))
    local = spec((1, N, wide), lambda g, k: (k, 0, g))
    local_r = spec((1, N, wide), lambda g, k: (nk - 1 - k, 0, g))
    end = spec((2, N, wide), lambda g, k: (0, 0, g))
    rowed = spec((per, C), lambda g, k: (g, k))

    states, pulls, ends = pl.pallas_call(
        functools.partial(state_kernel, per),
        grid=(groups, nk),
        in_specs=[big, big_r, small, small_r, small, small_r, line, line_r],
        out_specs=(local, local_r, end),
        out_shape=(
            jax.ShapeDtypeStruct((nk, N, width), F32),
            jax.ShapeDtypeStruct((nk, N, width), F32),
            jax.ShapeDtypeStruct((2, N, width), F32),
        ),
        scratch_shapes=[pltpu.VMEM((N, wide), F32), pltpu.VMEM((N, wide), F32)],
        compiler_params=params(),
        cost_estimate=pl.CostEstimate(flops=8 * length * width * N, bytes_accessed=24 << 20, transcendentals=0),
        name="states",
    )(signal, grad_out, input_map, output_map, col, col, tot, tot)

    inner_shapes = (
        jax.ShapeDtypeStruct((length, width), F32),
        jax.ShapeDtypeStruct((length, groups * N), F32),
        jax.ShapeDtypeStruct((length, groups * N), F32),
        jax.ShapeDtypeStruct((length, groups * C), F32),
        jax.ShapeDtypeStruct((nk, 1, width), F32),
    )
    def inner(first, each, carried):
        def moved(shape, kind):
            if kind == "tok":
                return spec(shape, lambda g, k: (first + k, g))
            if kind == "row":
                return spec(shape, lambda g, k: (g, first + k))
            return spec(shape, lambda g, k: (first + k, 0, g))

        b, s = moved((C, wide), "tok"), moved((C, C), "tok")
        return pl.pallas_call(
            functools.partial(inner_kernel, per, len(carried)),
            grid=(groups, each),
            in_specs=[b, b, s, s, s, moved((per, C), "row")]
            + [pl.BlockSpec(memory_space=pl.ANY)] * len(carried),
            out_specs=(b, s, s, s, moved((1, 1, wide), "line")),
            out_shape=inner_shapes,
            input_output_aliases={6 + i: i for i in range(len(carried))},
            compiler_params=params(),
            cost_estimate=pl.CostEstimate(
                flops=8_000_000_000 * each // nk * 4, bytes_accessed=(16 << 20) * each // nk, transcendentals=0
            ),
            name="inner",
        )(signal, grad_out, input_map, output_map, col, row, *carried)

    count = lax.axis_size("ctx")
    hops = count // (2 if count < 16 else 4) + 1
    marks = [round(i * nk / hops) for i in range(hops + 1)]

    def stage(i):
        def run(carried):
            first, each = marks[i], marks[i + 1] - marks[i]
            return inner(first, each, carried) if each else carried

        return run

    fade = jnp.repeat(jnp.exp(jnp.sum(sums, axis=1)), P_SIZE)[None, :]
    carried_ends, carried = carry(ends, fade, [stage(i) for i in range(hops)], ())
    z, gq, gk, r, skip = carried

    grad_skip = lax.psum(jnp.sum(skip.reshape(nk, heads, P_SIZE), axis=(0, 2)), "ctx")

    grad_signal, grad_step, grad_decay, grad_input, grad_output = pl.pallas_call(
        functools.partial(outer_kernel, per),
        grid=(groups, nk),
        in_specs=[big, big, small, small, small, rowed, local, local, end, line, line, line,
                  spec((1, wide), lambda g, k: (0, g)), big, small, small, small],
        out_specs=(big, rowed, rowed, small, small),
        out_shape=(
            jax.ShapeDtypeStruct((length, width), BF16),
            jax.ShapeDtypeStruct((heads, length), F32),
            jax.ShapeDtypeStruct((heads, length), F32),
            jax.ShapeDtypeStruct((length, groups * N), BF16),
            jax.ShapeDtypeStruct((length, groups * N), BF16),
        ),
        compiler_params=params(),
        cost_estimate=pl.CostEstimate(flops=16 * length * width * N, bytes_accessed=40 << 20, transcendentals=0),
        name="outer",
    )(signal, grad_out, input_map, output_map, col, step_size, states, pulls, carried_ends,
      pre, post, tot, gains, z, gq, gk, r)
    return (grad_signal, grad_step, grad_decay, grad_input, grad_output, grad_skip)


def solution(mesh):
    placed = (
        P("ctx", "head"),
        P("head", "ctx"),
        P("head", "ctx"),
        P("ctx", "head"),
        P("ctx", "head"),
        P("head"),
        P("ctx", "head"),
    )
    return jax.shard_map(
        on_device,
        mesh=mesh,
        in_specs=placed,
        out_specs=(
            P("ctx", "head"),
            P("head", "ctx"),
            P("head", "ctx"),
            P("ctx", "head"),
            P("ctx", "head"),
            P("head"),
        ),
        check_vma=False,
    )
```

time: 541 us -> 210 us (0.39); the launches traced: 533 us -> 208 us
  matrix products: 156 us -> 0 us
  Pallas kernels: 0 us -> 126 us
  other arithmetic: 137 us -> 11.8 us
  local copies, waits for them, and re-layouts: 120 us -> 20.3 us
  waiting for transfers between devices: 61.7 us -> 17.2 us
  blocking collectives: 41.3 us -> 20.4 us
  between operations: 14.8 us -> 1.13 us
  starting transfers between devices: 0.26 us -> 11.9 us
    dot_general x15 -> x0, matrix products: 156 us -> none  [the longest x2 53.9 us: block_forward(): inner = jnp.einsum('ghkqs,ksghp->kqghp', weights, tokens, precision=HIGH)]
    pallas_call x0 -> x8, Pallas kernels: none -> 126 us  [the longest x5 54.6 us: inner(): pl.pallas_call(functools.partial(inner_kernel, per, len(carried)), grid=(...]
    another operation x12 -> x5, other arithmetic: 74.2 us -> 5.21 us  [the longest x2 3.51 us: carry(): both = jnp.stack(by_sender(got, nx, x), axis=1)]
    all_gather x2 -> x0, waiting for transfers between devices: 61.6 us -> none  [carried_in(): gathered = jax.tree.map(lambda a: lax.all_gather(a, axis), part)]
    another operation x30 -> x5, local copies, waits for them, and re-layouts: 48 us -> 2.35 us  [the longest x3 2.18 us: lanes(): return jnp.repeat(jnp.exp(a.T), P_SIZE, axis=1)[:, None, :]]
    unnamed x52 -> x61, local copies, waits for them, and re-layouts: 45.3 us -> 14.4 us
    ppermute x0 -> x9, waiting for transfers between devices: none -> 17.2 us  [the longest x2 10.8 us: exchange(): got.append(lax.ppermute(sent, 'ctx', pairs))]
    all_gather x1 -> x0, blocking collectives: 16.9 us -> none  [carried_in(): gathered = jax.tree.map(lambda a: lax.all_gather(a, axis), part)]
  transfers between devices with their start and end apart: 2 -> 9, of which waited for: 1 -> 4; matrix products, arithmetic and copies ran while one was open for 28% -> 3% of each run, Pallas kernels for 0% -> 37%
where the time goes in v1:
time: 210 us; the launch traced here: 208 us
  Pallas kernels  126 us (60%)
  blocking collectives  20.4 us (10%)
  local copies, waits for them, and re-layouts  20.3 us (10%)
  waiting for transfers between devices  17.2 us (8%)
  starting transfers between devices  11.9 us (6%)
  other arithmetic  11.8 us (6%)
    pallas_call x5, Pallas kernels, inner(): pl.pallas_call(functools.partial(inner_kernel, per, len(carried)), grid=(...  54.6 us
    pallas_call x1, Pallas kernels, on_device(): pl.pallas_call(functools.partial(outer_kernel, per), grid=(groups, nk), i...  48.7 us
    pallas_call x1, Pallas kernels, on_device(): pl.pallas_call(functools.partial(state_kernel, per), grid=(groups, nk), i...  20.9 us
    psum x1, blocking collectives, on_device(): lax.psum(jnp.sum(skip.reshape(nk, heads, P_SIZE), axis=(0, 2)), 'ctx')  20.4 us
    unnamed x61, local copies, waits for them, and re-layouts  14.4 us
    ppermute x2, waiting for transfers between devices, exchange(): got.append(lax.ppermute(sent, 'ctx', pairs))  10.8 us
    ppermute x3, starting transfers between devices, carry(): lax.ppermute(up_send, 'ctx', up)  5.68 us
  transfers between devices with their start and end apart: 9, of which 4 were waited for; matrix products, arithmetic and copies ran while one was open for 3% of the time, Pallas kernels for 37%

profile of v1, /device:TPU:0, one launch (start us, length us, event | category | flops | bytes accessed | tf_op | source)
XLA Modules:
  0.0 208.5 jit_solution(8129318432311081370)
XLA Ops:
  1.8 3.0 %collective-permute-start = (f32[1,2048]{1,0:T(1,128)S(1)}, f32[1,2048]{1,0:T(1,128)S(1)}, u32[]{:S(2)}, u32[]{:S(2)}) collective-permute-start(f32[1,2048]{1,0:T(1,128)S(1)} %broadcast_in_dim_reshape.16), channel_id=1, source_target_pairs={{0,4},{4,0},{8,12},{12,8},{16,20},{20,16},{24,28},{28,24},{1,5},{5... | collective-permute-start | bytes 24584 | tf_op jit(solution)/shard_map/ppermute | solution.py:228
  8.0 1.6 prep.1
  11.7 20.9 %states.1 = (f32[8,128,2048]{2,1,0:T(8,128)}, f32[8,128,2048]{2,1,0:T(8,128)}, f32[2,128,2048]{2,1,0:T(8,128)S(1)}) custom-call(bf16[1024,2048]{1,0:T(8,128)(2,1)} %x_ref.13, bf16[1024,2048]{1,0:T(8,128)(2,1)} %dy_ref.13, bf16[1024,256]{1,0:T(8,128)(2,1)S(1)} %copy-done.8, bf16[1024,256]{1,0:T(8,128)(2,1)S(1)} %copy-done.14, ...), custom_call_target="tpu_custom_call" | custom-call | flops 2147483648 | bytes 25165824 | tf_op jit(solution)/shard_map/states/pallas_call | solution.py:309
  32.6 1.5 dynamic-slice_bitcast_fusion
  34.1 13.2 %inner.5 = (f32[1024,2048]{1,0:T(8,128)}, f32[1024,256]{1,0:T(8,128)S(1)}, f32[1024,256]{1,0:T(8,128)S(1)}, f32[1024,256]{1,0:T(8,128)S(1)}, f32[8,1,2048]{2,1,0:T(1,128)S(1)}) custom-call(bf16[1024,2048]{1,0:T(8,128)(2,1)} %x_ref.13, bf16[1024,2048]{1,0:T(8,128)(2,1)} %dy_ref.13, bf16[1024,256]{1,0:T(8,128)(2,1)S(1)} %copy-done.9, ...), custom_call_target="tpu_custom_call" | custom-call | flops 8000000000 | bytes 4194304 | tf_op jit(solution)/shard_map/inner/pallas_call | solution.py:341
  48.3 10.7 %collective-permute-done.1 = f32[2,64,2048]{2,1,0:T(8,128)} collective-permute-done((f32[2,64,2048]{2,1,0:T(8,128)}, f32[2,64,2048]{2,1,0:T(8,128)}, u32[]{:S(2)}, u32[]{:S(2)}) %collective-permute-start.1) | collective-permute-done | bytes 1048608 | tf_op jit(solution)/shard_map/ppermute | solution.py:203
  59.0 1.8 broadcast_select_fusion
  61.7 3.5 %collective-permute-start.2 = (f32[64,2048]{1,0:T(8,128)S(1)}, f32[64,2048]{1,0:T(8,128)S(1)}, u32[]{:S(2)}, u32[]{:S(2)}) collective-permute-start(f32[64,2048]{1,0:T(8,128)S(1)} %get-tuple-element.160), channel_id=1, source_target_pairs={{0,8},{4,12},{1,9},{5,13},{2,10},{6,14},{3,11},{7,15}} | collective-permute-start | bytes 1572872 | tf_op jit(solution)/shard_map/ppermute | solution.py:247
  65.2 7.5 %inner.6 = (f32[1024,2048]{1,0:T(8,128)}, f32[1024,256]{1,0:T(8,128)S(1)}, f32[1024,256]{1,0:T(8,128)S(1)}, f32[1024,256]{1,0:T(8,128)S(1)}, f32[8,1,2048]{2,1,0:T(1,128)S(1)}) custom-call(bf16[1024,2048]{1,0:T(8,128)(2,1)} %x_ref.13, bf16[1024,2048]{1,0:T(8,128)(2,1)} %dy_ref.13, ...), custom_call_target="tpu_custom_call", output_to_operand_aliasing={{0}: (6, {}), {1}: (7, {}), {2}: (8, {}), {3}: (9, {}), {4}... | custom-call | flops 4000000000 | bytes 2097152 | tf_op jit(solution)/shard_map/inner/pallas_call | solution.py:341
  72.7 2.4 %collective-permute-done.2 = f32[64,2048]{1,0:T(8,128)S(1)} collective-permute-done((f32[64,2048]{1,0:T(8,128)S(1)}, f32[64,2048]{1,0:T(8,128)S(1)}, u32[]{:S(2)}, u32[]{:S(2)}) %collective-permute-start.2) | collective-permute-done | bytes 524320 | tf_op jit(solution)/shard_map/ppermute | solution.py:247
  76.7 13.2 %inner.7 = (f32[1024,2048]{1,0:T(8,128)}, f32[1024,256]{1,0:T(8,128)S(1)}, f32[1024,256]{1,0:T(8,128)S(1)}, f32[1024,256]{1,0:T(8,128)S(1)}, f32[8,1,2048]{2,1,0:T(1,128)S(1)}) custom-call(bf16[1024,2048]{1,0:T(8,128)(2,1)} %x_ref.13, bf16[1024,2048]{1,0:T(8,128)(2,1)} %dy_ref.13, ...), custom_call_target="tpu_custom_call", output_to_operand_aliasing={{0}: (6, {}), {1}: (7, {}), {2}: (8, {}), {3}: (9, {}), {4}... | custom-call | flops 8000000000 | bytes 4194304 | tf_op jit(solution)/shard_map/inner/pallas_call | solution.py:341
  90.9 1.5 multiply_add_fusion
  92.3 1.3 collective-permute-start.7
  93.6 1.5 collective-permute-start.6
  95.3 1.2 copy-done.3
  98.6 7.6 %inner.8 = (f32[1024,2048]{1,0:T(8,128)}, f32[1024,256]{1,0:T(8,128)S(1)}, f32[1024,256]{1,0:T(8,128)S(1)}, f32[1024,256]{1,0:T(8,128)S(1)}, f32[8,1,2048]{2,1,0:T(1,128)S(1)}) custom-call(bf16[1024,2048]{1,0:T(8,128)(2,1)} %x_ref.13, bf16[1024,2048]{1,0:T(8,128)(2,1)} %dy_ref.13, ...), custom_call_target="tpu_custom_call", output_to_operand_aliasing={{0}: (6, {}), {1}: (7, {}), {2}: (8, {}), {3}: (9, {}), {4}... | custom-call | flops 4000000000 | bytes 2097152 | tf_op jit(solution)/shard_map/inner/pallas_call | solution.py:341
  106.3 3.9 %collective-permute-done.7 = f32[64,2048]{1,0:T(8,128)} collective-permute-done((f32[64,2048]{1,0:T(8,128)}, f32[64,2048]{1,0:T(8,128)}, u32[]{:S(2)}, u32[]{:S(2)}) %collective-permute-start.7) | collective-permute-done | bytes 524320 | tf_op jit(solution)/shard_map/ppermute | solution.py:247
  110.2 1.5 add_bitcast_fusion
  111.9 1.6 fusion.1
  121.0 13.2 %inner.9 = (f32[1024,2048]{1,0:T(8,128)}, f32[1024,256]{1,0:T(8,128)S(1)}, f32[1024,256]{1,0:T(8,128)S(1)}, f32[1024,256]{1,0:T(8,128)S(1)}, f32[8,1,2048]{2,1,0:T(1,128)S(1)}) custom-call(bf16[1024,2048]{1,0:T(8,128)(2,1)} %x_ref.13, bf16[1024,2048]{1,0:T(8,128)(2,1)} %dy_ref.13, ...), custom_call_target="tpu_custom_call", output_to_operand_aliasing={{0}: (6, {}), {1}: (7, {}), {2}: (8, {}), {3}: (9, {}), {4}... | custom-call | flops 8000000000 | bytes 4194304 | tf_op jit(solution)/shard_map/inner/pallas_call | solution.py:341
  135.6 20.4 %psum.7 = f32[32]{0:T(128)} all-reduce(f32[32]{0:T(128)S(1)} %reduce_sum.58), channel_id=1, replica_groups=mesh['ctx'=8,'head'=4] {'ctx'}, use_global_device_ids=true, to_apply=%region_6.7 | all-reduce | flops 32 | bytes 256 | tf_op jit(solution)/shard_map/psum | solution.py:371
  156.0 1.9 select_bitcast_fusion.1
  157.9 1.6 pad_maximum_fusion
  159.6 48.7 %outer.1 = (bf16[1024,2048]{1,0:T(8,128)(2,1)}, f32[32,1024]{1,0:T(8,128)}, f32[32,1024]{1,0:T(8,128)}, bf16[1024,256]{1,0:T(8,128)(2,1)}, bf16[1024,256]{1,0:T(8,128)(2,1)}) custom-call(bf16[1024,2048]{1,0:T(8,128)(2,1)} %x_ref.13, bf16[1024,2048]{1,0:T(8,128)(2,1)} %dy_ref.13, bf16[1024,256]{1,0:T(8,128)(2,1)S(1)} %copy-done.13, ...), custom_call_target="tpu_custom_call" | custom-call | flops 4294967296 | bytes 41943040 | tf_op jit(solution)/shard_map/outer/pallas_call | solution.py:373
  (99 shorter events, 22.3 us)
Async XLA Ops:
  1.8 46.4 %collective-permute-start = (f32[1,2048]{1,0:T(1,128)S(1)}, f32[1,2048]{1,0:T(1,128)S(1)}, u32[]{:S(2)}, u32[]{:S(2)}) collective-permute-start(f32[1,2048]{1,0:T(1,128)S(1)} %broadcast_in_dim_reshape.16), channel_id=1, source_target_pairs={{0,4},{4,0},{8,12},{12,8},{16,20},{20,16},{24,28},{28,24},{1,5},{5... | collective-permute-start | bytes 24584 | tf_op jit(solution)/shard_map/ppermute | solution.py:228
  34.1 24.9 %collective-permute-start.1 = (f32[2,64,2048]{2,1,0:T(8,128)}, f32[2,64,2048]{2,1,0:T(8,128)}, u32[]{:S(2)}, u32[]{:S(2)}) collective-permute-start(f32[2,64,2048]{2,1,0:T(8,128)} %get-tuple-element.163), channel_id=1, source_target_pairs={{0,4},{4,0},{8,12},{12,8},{16,20},{20,16},{24,28},{28,24},{1,5},{5... | collective-permute-start | bytes 3145736 | tf_op jit(solution)/shard_map/ppermute | solution.py:203
  48.3 16.9 %copy-start.1 = (f32[1024,256]{1,0:T(8,128)S(1)}, f32[1024,256]{1,0:T(8,128)}, u32[]{:S(2)}) copy-start(f32[1024,256]{1,0:T(8,128)} %copy-done) | copy-start | bytes 3145732
  48.3 16.9 %copy-start.10 = (bf16[1024,256]{1,0:T(8,128)(2,1)S(1)}, bf16[1024,256]{1,0:T(8,128)(2,1)}, u32[]{:S(2)}) copy-start(bf16[1024,256]{1,0:T(8,128)(2,1)} %k_ref.13) | copy-start | bytes 1572868
  48.3 16.9 %copy-start.16 = (bf16[1024,256]{1,0:T(8,128)(2,1)S(1)}, bf16[1024,256]{1,0:T(8,128)(2,1)}, u32[]{:S(2)}) copy-start(bf16[1024,256]{1,0:T(8,128)(2,1)} %q_ref.13) | copy-start | bytes 1572868
  60.8 11.9 %copy-start.23 = (f32[2,64,2048]{2,1,0:T(8,128)}, f32[2,64,2048]{2,1,0:T(8,128)S(1)}, u32[]{:S(2)}) copy-start(f32[2,64,2048]{2,1,0:T(8,128)S(1)} %get-tuple-element.161) | copy-start | bytes 3145732
  60.8 11.9 %copy-start.25 = (f32[2,64,2048]{2,1,0:T(8,128)}, f32[2,64,2048]{2,1,0:T(8,128)S(1)}, u32[]{:S(2)}) copy-start(f32[2,64,2048]{2,1,0:T(8,128)S(1)} %get-tuple-element.162) | copy-start | bytes 3145732
  61.0 11.7 %collective-permute-start.3 = (f32[64,2048]{1,0:T(8,128)S(1)}, f32[64,2048]{1,0:T(8,128)S(1)}, u32[]{:S(2)}, u32[]{:S(2)}) collective-permute-start(f32[64,2048]{1,0:T(8,128)S(1)} %get-tuple-element.159), channel_id=1, source_target_pairs={{24,16},{28,20},{25,17},{29,21},{26,18},{30,22},{27,19},{31,23}} | collective-permute-start | bytes 1572872 | tf_op jit(solution)/shard_map/ppermute | solution.py:247
  61.7 13.5 %collective-permute-start.2 = (f32[64,2048]{1,0:T(8,128)S(1)}, f32[64,2048]{1,0:T(8,128)S(1)}, u32[]{:S(2)}, u32[]{:S(2)}) collective-permute-start(f32[64,2048]{1,0:T(8,128)S(1)} %get-tuple-element.160), channel_id=1, source_target_pairs={{0,8},{4,12},{1,9},{5,13},{2,10},{6,14},{3,11},{7,15}} | collective-permute-start | bytes 1572872 | tf_op jit(solution)/shard_map/ppermute | solution.py:247
  75.3 15.6 %collective-permute-start.5 = (f32[64,2048]{1,0:T(8,128)S(1)}, f32[64,2048]{1,0:T(8,128)S(1)}, u32[]{:S(2)}, u32[]{:S(2)}) collective-permute-start(f32[64,2048]{1,0:T(8,128)S(1)} %get-tuple-element.171), channel_id=1, source_target_pairs={{16,8},{20,12},{17,9},{21,13},{18,10},{22,14},{19,11},{23,15}} | collective-permute-start | bytes 1572872 | tf_op jit(solution)/shard_map/ppermute | solution.py:247
  76.0 14.9 %collective-permute-start.4 = (f32[64,2048]{1,0:T(8,128)S(1)}, f32[64,2048]{1,0:T(8,128)S(1)}, u32[]{:S(2)}, u32[]{:S(2)}) collective-permute-start(f32[64,2048]{1,0:T(8,128)S(1)} %get-tuple-element.172), channel_id=1, source_target_pairs={{8,16},{12,20},{9,17},{13,21},{10,18},{14,22},{11,19},{15,23}} | collective-permute-start | bytes 1572872 | tf_op jit(solution)/shard_map/ppermute | solution.py:247
  90.8 4.3 %copy-start.29 = (f32[32]{0:T(128)S(1)}, f32[32]{0:T(128)}, u32[]{:S(2)}) copy-start(f32[32]{0:T(128)} %param.12) | copy-start | bytes 388
  92.3 17.8 %collective-permute-start.7 = (f32[64,2048]{1,0:T(8,128)}, f32[64,2048]{1,0:T(8,128)}, u32[]{:S(2)}, u32[]{:S(2)}) collective-permute-start(f32[64,2048]{1,0:T(8,128)} %get-tuple-element.148), channel_id=1, source_target_pairs={{8,0},{12,4},{9,1},{13,5},{10,2},{14,6},{11,3},{15,7}} | collective-permute-start | bytes 1572872 | tf_op jit(solution)/shard_map/ppermute | solution.py:247
  93.6 16.5 %collective-permute-start.6 = (f32[64,2048]{1,0:T(8,128)}, f32[64,2048]{1,0:T(8,128)}, u32[]{:S(2)}, u32[]{:S(2)}) collective-permute-start(f32[64,2048]{1,0:T(8,128)} %get-tuple-element.169), channel_id=1, source_target_pairs={{16,24},{20,28},{17,25},{21,29},{18,26},{22,30},{19,27},{23,31}} | collective-permute-start | bytes 1572872 | tf_op jit(solution)/shard_map/ppermute | solution.py:247
  98.6 11.5 %copy-start.24 = (f32[2,64,2048]{2,1,0:T(8,128)S(1)}, f32[2,64,2048]{2,1,0:T(8,128)}, u32[]{:S(2)}) copy-start(f32[2,64,2048]{2,1,0:T(8,128)} %copy-done.23) | copy-start | bytes 3145732
  98.6 11.5 %copy-start.26 = (f32[2,64,2048]{2,1,0:T(8,128)S(1)}, f32[2,64,2048]{2,1,0:T(8,128)}, u32[]{:S(2)}) copy-start(f32[2,64,2048]{2,1,0:T(8,128)} %copy-done.25) | copy-start | bytes 3145732
  98.6 11.5 %copy-start.27 = (f32[64,2048]{1,0:T(8,128)S(1)}, f32[64,2048]{1,0:T(8,128)}, u32[]{:S(2)}) copy-start(f32[64,2048]{1,0:T(8,128)} %get-tuple-element.149) | copy-start | bytes 1572868
  98.6 11.5 %copy-start.28 = (f32[64,2048]{1,0:T(8,128)S(1)}, f32[64,2048]{1,0:T(8,128)}, u32[]{:S(2)}) copy-start(f32[64,2048]{1,0:T(8,128)} %get-tuple-element.170) | copy-start | bytes 1572868
  106.3 5.6 %copy-start.4 = (f32[1024,256]{1,0:T(8,128)}, f32[1024,256]{1,0:T(8,128)S(1)}, u32[]{:S(2)}) copy-start(f32[1024,256]{1,0:T(8,128)S(1)} %get-tuple-element.127.rest_3_) | copy-start | bytes 3145732
  113.5 21.9 %collective-permute-start.8 = (f32[2,64,2048]{2,1,0:T(8,128)}, f32[2,64,2048]{2,1,0:T(8,128)}, u32[]{:S(2)}, u32[]{:S(2)}) collective-permute-start(f32[2,64,2048]{2,1,0:T(8,128)} %get-tuple-element.157), channel_id=1, source_target_pairs={{0,4},{4,0},{8,12},{12,8},{16,20},{20,16},{24,28},{28,24},{1,5},{5... | collective-permute-start | bytes 3145736 | tf_op jit(solution)/shard_map/ppermute | solution.py:203
  156.0 3.5 %copy-start.7 = (f32[1024,256]{1,0:T(8,128)S(1)}, f32[1024,256]{1,0:T(8,128)}, u32[]{:S(2)}) copy-start(f32[1024,256]{1,0:T(8,128)} %copy-done.6) | copy-start | bytes 3145732
  156.0 3.5 %copy-start.13 = (bf16[1024,256]{1,0:T(8,128)(2,1)S(1)}, bf16[1024,256]{1,0:T(8,128)(2,1)}, u32[]{:S(2)}) copy-start(bf16[1024,256]{1,0:T(8,128)(2,1)} %k_ref.13) | copy-start | bytes 1572868
  156.0 3.5 %copy-start.19 = (bf16[1024,256]{1,0:T(8,128)(2,1)S(1)}, bf16[1024,256]{1,0:T(8,128)(2,1)}, u32[]{:S(2)}) copy-start(bf16[1024,256]{1,0:T(8,128)(2,1)} %q_ref.13) | copy-start | bytes 1572868
  156.0 3.5 %copy-start.22 = (f32[32,1024]{1,0:T(8,128)S(1)}, f32[32,1024]{1,0:T(8,128)}, u32[]{:S(2)}) copy-start(f32[32,1024]{1,0:T(8,128)} %step_ref.3) | copy-start | bytes 393220
  (15 other events, 16.6 us)

commit v2 on v1

v2 whole, which is shorter than its diff:
```python
import functools

import jax
import jax.numpy as jnp
from jax import lax
from jax.experimental import pallas as pl
from jax.experimental.pallas import tpu as pltpu
from jax.sharding import PartitionSpec as P

P_SIZE = 64
N = 128
C = 128
LOG2E = 1.4426950408889634
F32 = jnp.float32
BF16 = jnp.bfloat16
NT = (((1,), (1,)), ((), ()))
TN = (((0,), (0,)), ((), ()))
NN = (((1,), (0,)), ((), ()))


def dot(a, b, dims):
    return lax.dot_general(a, b, dims, preferred_element_type=F32)


def split(a):
    high = a.astype(BF16)
    return high, (a - high.astype(F32)).astype(BF16)


def halves():
    lane = lax.broadcasted_iota(jnp.int32, (1, 2 * P_SIZE), 1)
    low = (lane < P_SIZE).astype(F32)
    return low, 1.0 - low


def blocks_of(pair):
    low, high = halves()
    return jnp.concatenate([pair * low.astype(pair.dtype), pair * high.astype(pair.dtype)], axis=0)


def params(**more):
    return pltpu.CompilerParams(vmem_limit_bytes=48 * 1024 * 1024, **more)


def prep_kernel(groups, per, decay_ref, step_ref, col_ref, row_ref):
    heads = decay_ref.shape[0]
    lane = lax.broadcasted_iota(jnp.int32, (heads, C), 1)
    for k in range(decay_ref.shape[1] // C):
        at = slice(k * C, (k + 1) * C)
        step = step_ref[:, at]
        cum = decay_ref[:, at]
        shift = 1
        while shift < C:
            cum = cum + jnp.where(lane >= shift, pltpu.roll(cum, shift, 1), 0.0)
            shift *= 2
        total = cum[:, C - 1 :]
        cum2 = cum * LOG2E
        low2 = cum2 - jnp.log(step) * LOG2E
        rise = jnp.exp(cum)
        tail = jnp.exp(total - cum) * step
        for g in range(groups):
            own = slice(g * per, (g + 1) * per)
            pad = jnp.zeros((C - 3 * per, C), F32)
            stacked = jnp.concatenate([low2[own], rise[own], tail[own], pad], axis=0)
            rows = jnp.concatenate([cum2[own], rise[own], tail[own]], axis=0)
            row_ref[g * 3 * per : (g + 1) * 3 * per, at] = rows
            col_ref[at, g * C : (g + 1) * C] = stacked.T


def state_kernel(per, x_ref, dy_ref, k_ref, q_ref, col_ref, tot_ref, pre_ref,
                 h_ref, u_ref, ends_ref, skip_ref, h_s, g_s):
    k = pl.program_id(1)

    @pl.when(k == 0)
    def _():
        h_s[...] = jnp.zeros_like(h_s)
        g_s[...] = jnp.zeros_like(g_s)
        skip_ref[...] = jnp.zeros_like(skip_ref)

    low, _ = halves()
    keys = jnp.concatenate([k_ref[...]] * 2, axis=0)
    queries = jnp.concatenate([q_ref[...]] * 2, axis=0)
    col = col_ref[...]

    def scaled(ref, first):
        parts = []
        for j in range(per // 2):
            a = first + 2 * j
            factor = jnp.where(low > 0, col[:, a : a + 1], col[:, a + 1 : a + 2])
            parts.append(ref[:, 128 * j : 128 * (j + 1)].astype(F32) * factor)
        return jnp.concatenate(split(jnp.concatenate(parts, axis=1)), axis=0)

    h_ref[0] = h_s[...]
    h_s[...] = tot_ref[0] * h_s[...] + dot(keys, scaled(x_ref, 2 * per), TN)
    pull = dot(queries, scaled(dy_ref, per), TN)
    u_ref[0] = pull
    g_s[...] = g_s[...] + pre_ref[0] * pull
    both = x_ref[...].astype(F32) * dy_ref[...].astype(F32)
    skip_ref[...] = skip_ref[...] + jnp.sum(both, axis=0, keepdims=True)

    @pl.when(k == pl.num_programs(1) - 1)
    def _():
        ends_ref[0] = h_s[...]
        ends_ref[1] = g_s[...]


def inner_kernel(per, carried, x_ref, dy_ref, k_ref, q_ref, col_ref, row_ref, *rest):
    z_ref, gq_ref, gk_ref, rc_ref, c_s = rest[carried:]
    mask = lax.broadcasted_iota(jnp.int32, (C, C), 1) >= lax.broadcasted_iota(jnp.int32, (C, C), 0)
    keys = k_ref[...]
    queries = q_ref[...]
    scores = dot(keys, queries, NT)
    total = jnp.zeros((C, C), F32)
    for j in range(per // 2):
        at = slice(128 * j, 128 * (j + 1))
        ups = blocks_of(dy_ref[:, at])
        met = dot(x_ref[:, at], ups, NT)
        highs, lows = [], []
        for i in range(2):
            a = 2 * j + i
            spread = jnp.where(mask, row_ref[a : a + 1, :] - col_ref[:, a : a + 1], -1e4)
            decay = jnp.exp2(spread)
            lm = decay * met[:, i * C : (i + 1) * C]
            total = total + lm
            both = lm * scores
            rc_ref[a : a + 1, :] = jnp.sum(both, axis=0, keepdims=True)
            c_s[:, a : a + 1] = jnp.sum(both, axis=1, keepdims=True)
            high, rest_of = split(decay * scores)
            highs.append(high)
            lows.append(rest_of)
        z_ref[:, at] = dot(jnp.concatenate(highs, axis=1), ups, NN) + dot(
            jnp.concatenate(lows, axis=1), ups, NN
        )
    high, rest_of = split(total)
    gq_ref[...] = dot(high, keys, TN) + dot(rest_of, keys, TN)
    gk_ref[...] = dot(high, queries, NN) + dot(rest_of, queries, NN)
    rc_ref[per:, :] = c_s[...].T[:per]


def outer_kernel(per, nx, x_ref, dy_ref, k_ref, q_ref, col_ref, row_ref, step_ref, h_ref, u_ref,
                 tot_ref, pre_ref, gain_ref, z_ref, gq_ref, gk_ref, rc_ref, *rest):
    got = rest[:nx]
    gx_ref, gstep_ref, gdecay_ref, gkey_ref, gquery_ref, e_s, g_s, r_s, c_s, edge_s = rest[nx:]
    place = lax.rem(lax.axis_index("ctx"), nx)

    @pl.when(pl.program_id(1) == 0)
    def _():
        size = N // nx
        for r in range(nx):
            part = pl.ds(pl.multiple_of(lax.rem(place - r + nx, nx) * size, size), size)
            e_s[part, :] = got[r][0]
            g_s[part, :] = got[r][1]

    low, high_half = halves()
    keys2 = jnp.concatenate([k_ref[...]] * 2, axis=1)
    keys_t = k_ref[...].astype(F32).T
    queries_t = q_ref[...].astype(F32).T
    gq = jnp.zeros((N, C), F32)
    gk = jnp.zeros((N, C), F32)
    for j in range(per // 2):
        at = slice(128 * j, 128 * (j + 1))
        x = x_ref[:, at]
        dy = dy_ref[:, at]
        pull = g_s[:, at]
        tot = tot_ref[0, :, at]
        state = h_ref[0, :, at] + pre_ref[0, :, at] * e_s[:, at]
        g_s[:, at] = tot * pull + u_ref[0, :, at]
        edge = jnp.sum(state * pull, axis=0, keepdims=True) * tot
        s_high, s_low = split(state)
        p_high, p_low = split(pull)
        s_both = jnp.concatenate([blocks_of(s_high), blocks_of(s_low)], axis=1)
        p_both = jnp.concatenate([blocks_of(p_high), blocks_of(p_low)], axis=1)
        to_q = dot(s_both, jnp.concatenate([dy, dy], axis=1), NT)
        to_k = dot(p_both, jnp.concatenate([x, x], axis=1), NT)
        z_out = dot(keys2, jnp.concatenate([p_high, p_low], axis=0), NN)
        a = 2 * j
        tails = [col_ref[:, 2 * per + a + i : 2 * per + a + i + 1] for i in range(2)]
        z = z_ref[:, at] + z_out * jnp.where(low > 0, tails[0], tails[1])
        gx_ref[:, at] = (z + gain_ref[0, :, at] * dy.astype(F32)).astype(BF16)
        for i, half in enumerate((low, high_half)):
            own_q = to_q[i * N : (i + 1) * N] * row_ref[per + a + i : per + a + i + 1, :]
            own_k = to_k[i * N : (i + 1) * N] * row_ref[2 * per + a + i : 2 * per + a + i + 1, :]
            gq = gq + own_q
            gk = gk + own_k
            r_s[a + i : a + i + 1, :] = jnp.sum(own_q * queries_t, axis=0, keepdims=True)
            c_s[a + i : a + i + 1, :] = jnp.sum(own_k * keys_t, axis=0, keepdims=True)
            edge_s[a + i : a + i + 1, :] = edge * half
    gquery_ref[...] = (gq_ref[...] + gq.T).astype(BF16)
    gkey_ref[...] = (gk_ref[...] + gk.T).astype(BF16)
    cols = rc_ref[per:, :] + c_s[...]
    part = rc_ref[:per, :] + r_s[...] - cols
    edge_sum = jnp.sum(edge_s[...] + c_s[...], axis=1, keepdims=True)
    lane = lax.broadcasted_iota(jnp.int32, (per, C), 1)
    part = jnp.where(lane == C - 1, part + edge_sum, part)
    shift = 1
    while shift < C:
        part = part + jnp.where(lane < C - shift, pltpu.roll(part, C - shift, 1), 0.0)
        shift *= 2
    gdecay_ref[...] = part
    gstep_ref[...] = cols / step_ref[...]


def exchange(parts, nx, x, nz):
    kept = lax.dynamic_index_in_dim(parts, x, 1, False)
    got = [kept]
    for r in range(1, nx):
        pairs = [(c * nx + i, c * nx + (i + r) % nx) for c in range(nz) for i in range(nx)]
        sent = lax.dynamic_index_in_dim(parts, (x + r) % nx, 1, False)
        got.append(lax.ppermute(sent, "ctx", pairs))
    return got


def by_sender(got, nx, x):
    out = []
    for j in range(nx):
        one = got[0]
        for r in range(1, nx):
            one = jnp.where((x - j) % nx == r, got[r], one)
        out.append(one)
    return out


def held(value, work):
    return lax.optimization_barrier((value, work))


def carry(ends, fade, skip, stages, work):
    count = lax.axis_size("ctx")
    nx = 2 if count < 16 else 4
    nz = count // nx
    place = lax.axis_index("ctx")
    x, z = place % nx, place // nx
    turns = [[(c * nx + i, c * nx + (i + r) % nx) for c in range(nz) for i in range(nx)] for r in range(nx)]
    line = jnp.concatenate([fade, skip], axis=0)
    lines = [line] + [lax.ppermute(line, "ctx", t) for t in turns[1:]]
    _, rows, width = ends.shape
    got = exchange(ends.reshape(2, nx, rows // nx, width), nx, x, nz)
    work = stages[0](work)
    (got, lines), work = held((got, lines), work)
    lines = by_sender(lines, nx, x)
    row_fade = [one[:1] for one in lines]
    all_fade = functools.reduce(lambda a, b: a * b, row_fade)
    skip = functools.reduce(lambda a, b: a + b, [one[1:] for one in lines])
    skips = [skip]
    for r in range(1, nz):
        skips.append(lax.ppermute(skip, "ctx", [(c * nx + i, (c + r) % nz * nx + i) for c in range(nz) for i in range(nx)]))
    both = by_sender(got, nx, x)
    states, pulls = [b[0] for b in both], [b[1] for b in both]
    state_sum = states[0]
    for i in range(1, nx):
        state_sum = row_fade[i] * state_sum + states[i]
    pull_sum = pulls[nx - 1]
    for i in range(nx - 2, -1, -1):
        pull_sum = row_fade[i] * pull_sum + pulls[i]
    entering, leaving, up_send, down_send = None, None, state_sum, pull_sum
    for hop in range(nz - 1):
        up = [(hop * nx + i, (hop + 1) * nx + i) for i in range(nx)]
        down = [((nz - 1 - hop) * nx + i, (nz - 2 - hop) * nx + i) for i in range(nx)]
        came = (lax.ppermute(up_send, "ctx", up), lax.ppermute(down_send, "ctx", down))
        work = stages[1 + hop](work)
        if hop == 0:
            (came, skips), work = held((came, skips), work)
            skip = functools.reduce(lambda a, b: a + b, by_sender(skips, nz, z))
        else:
            came, work = held(came, work)
        entering = came[0] if hop == 0 else entering + came[0]
        leaving = came[1] if hop == 0 else leaving + came[1]
        up_send = all_fade * entering + state_sum
        down_send = all_fade * leaving + pull_sum
    ins, outs = [entering], [leaving]
    for i in range(nx - 1):
        ins.append(row_fade[i] * ins[-1] + states[i])
    for i in range(nx - 1, 0, -1):
        outs.append(row_fade[i] * outs[-1] + pulls[i])
    got = exchange(jnp.stack([jnp.stack(ins), jnp.stack(outs[::-1])]), nx, x, nz)
    work = stages[nz](work)
    got, work = held(got, work)
    return got, skip, work


def on_device(signal, step_size, log_decay, input_map, output_map, skip_gain, grad_out):
    heads, length = step_size.shape
    groups = input_map.shape[1] // N
    per = heads // groups
    wide = per * P_SIZE
    width = heads * P_SIZE
    nk = length // C

    col, row = pl.pallas_call(
        functools.partial(prep_kernel, groups, per),
        out_shape=(
            jax.ShapeDtypeStruct((length, groups * C), F32),
            jax.ShapeDtypeStruct((3 * heads, length), F32),
        ),
        compiler_params=params(),
        name="prep",
    )(log_decay, step_size)

    sums = jnp.sum(log_decay.reshape(heads, nk, C), axis=-1)
    after = lax.broadcasted_iota(jnp.int32, (nk, nk), 0) < lax.broadcasted_iota(jnp.int32, (nk, nk), 1)
    before = jnp.sum(jnp.where(after[None], sums[:, :, None], 0.0), axis=1)
    span = jnp.sum(sums, axis=1)
    chunk_lines = jnp.exp(jnp.concatenate([sums.T, before.T, span[None]], axis=0))
    lines = jnp.concatenate([chunk_lines, skip_gain[None]], axis=0)
    lines = jnp.repeat(lines, P_SIZE, axis=1)[:, None, :]
    fade = lines[2 * nk]

    def spec(shape, index):
        return pl.BlockSpec(shape, index)

    def specs(at):
        return (
            spec((C, wide), lambda g, k: (at(k), g)),
            spec((C, C), lambda g, k: (at(k), g)),
            spec((1, N, wide), lambda g, k: (at(k), 0, g)),
            spec((1, 1, wide), lambda g, k: (at(k), 0, g)),
            spec((1, 1, wide), lambda g, k: (nk + at(k), 0, g)),
        )

    big, small, local, tot, pre = specs(lambda k: k)

    states, pulls, ends, skip = pl.pallas_call(
        functools.partial(state_kernel, per),
        grid=(groups, nk),
        in_specs=[big, big, small, small, small, tot, pre],
        out_specs=(local, local, spec((2, N, wide), lambda g, k: (0, 0, g)), spec((1, wide), lambda g, k: (0, g))),
        out_shape=(
            jax.ShapeDtypeStruct((nk, N, width), F32),
            jax.ShapeDtypeStruct((nk, N, width), F32),
            jax.ShapeDtypeStruct((2, N, width), F32),
            jax.ShapeDtypeStruct((1, width), F32),
        ),
        scratch_shapes=[pltpu.VMEM((N, wide), F32), pltpu.VMEM((N, wide), F32)],
        compiler_params=params(),
        cost_estimate=pl.CostEstimate(flops=8 * length * width * N, bytes_accessed=24 << 20, transcendentals=0),
        name="states",
    )(signal, grad_out, input_map, output_map, col, lines, lines)

    inner_shapes = (
        jax.ShapeDtypeStruct((length, width), F32),
        jax.ShapeDtypeStruct((length, groups * N), F32),
        jax.ShapeDtypeStruct((length, groups * N), F32),
        jax.ShapeDtypeStruct((2 * heads, length), F32),
    )
    def inner(first, each, carried):
        b, s, _, _, _ = specs(lambda k: first + k)
        return pl.pallas_call(
            functools.partial(inner_kernel, per, len(carried)),
            grid=(groups, each),
            in_specs=[b, b, s, s, s, spec((3 * per, C), lambda g, k: (g, first + k))]
            + [pl.BlockSpec(memory_space=pltpu.HBM)] * len(carried),
            out_specs=(b, s, s, spec((2 * per, C), lambda g, k: (g, first + k))),
            out_shape=inner_shapes,
            scratch_shapes=[pltpu.VMEM((C, C), F32)],
            input_output_aliases={6 + i: i for i in range(len(carried))},
            compiler_params=params(),
            cost_estimate=pl.CostEstimate(
                flops=8_000_000_000 * each // nk * 4, bytes_accessed=(16 << 20) * each // nk, transcendentals=0
            ),
            name="inner",
        )(signal, grad_out, input_map, output_map, col, row, *carried)

    count = lax.axis_size("ctx")
    hops = count // (2 if count < 16 else 4) + 1
    marks = [round(i * nk / hops) for i in range(hops + 1)]

    def stage(i):
        def run(carried):
            first, each = marks[i], marks[i + 1] - marks[i]
            return inner(first, each, carried) if each else carried

        return run

    got, skip, carried = carry(ends, fade, skip, [stage(i) for i in range(hops)], ())
    z, gq, gk, rc = carried
    nx = len(got)
    grad_skip = jnp.sum(skip.reshape(heads, P_SIZE), axis=1)

    def back(k):
        return nk - 1 - k

    big, small, local, tot, pre = specs(back)
    rowed = spec((per, C), lambda g, k: (g, back(k)))
    grad_signal, grad_step, grad_decay, grad_input, grad_output = pl.pallas_call(
        functools.partial(outer_kernel, per, nx),
        grid=(groups, nk),
        in_specs=[big, big, small, small, small, spec((3 * per, C), lambda g, k: (g, back(k))), rowed,
                  local, local, tot, pre, spec((1, 1, wide), lambda g, k: (2 * nk + 1, 0, g)),
                  big, small, small, spec((2 * per, C), lambda g, k: (g, back(k)))]
        + [spec((2, N // nx, wide), lambda g, k: (0, 0, g))] * nx,
        out_specs=(big, rowed, rowed, small, small),
        out_shape=(
            jax.ShapeDtypeStruct((length, width), BF16),
            jax.ShapeDtypeStruct((heads, length), F32),
            jax.ShapeDtypeStruct((heads, length), F32),
            jax.ShapeDtypeStruct((length, groups * N), BF16),
            jax.ShapeDtypeStruct((length, groups * N), BF16),
        ),
        scratch_shapes=[
            pltpu.VMEM((N, wide), F32),
            pltpu.VMEM((N, wide), F32),
            pltpu.VMEM((per, C), F32),
            pltpu.VMEM((per, C), F32),
            pltpu.VMEM((per, C), F32),
        ],
        compiler_params=params(),
        cost_estimate=pl.CostEstimate(flops=16 * length * width * N, bytes_accessed=40 << 20, transcendentals=0),
        name="outer",
    )(signal, grad_out, input_map, output_map, col, row, step_size, states, pulls,
      lines, lines, lines, z, gq, gk, rc, *got)
    return (grad_signal, grad_step, grad_decay, grad_input, grad_output, grad_skip)


def solution(mesh):
    placed = (
        P("ctx", "head"),
        P("head", "ctx"),
        P("head", "ctx"),
        P("ctx", "head"),
        P("ctx", "head"),
        P("head"),
        P("ctx", "head"),
    )
    return jax.shard_map(
        on_device,
        mesh=mesh,
        in_specs=placed,
        out_specs=(
            P("ctx", "head"),
            P("head", "ctx"),
            P("head", "ctx"),
            P("ctx", "head"),
            P("ctx", "head"),
            P("head"),
        ),
        check_vma=False,
    )
```

time: 210 us -> 162 us (0.77)
  Pallas kernels: 126 us -> 88.9 us
  blocking collectives: 20.4 us -> 0 us
  waiting for transfers between devices: 17.2 us -> 28.4 us
  local copies, waits for them, and re-layouts: 20.3 us -> 16.4 us
  starting transfers between devices: 11.9 us -> 15.6 us
    psum x1 -> x0, blocking collectives: 20.4 us -> none  [on_device(): lax.psum(jnp.sum(skip.reshape(nk, heads, P_SIZE), axis=(0, 2)), 'ctx')]
    pallas_call x1, Pallas kernels: 48.7 us -> 30.1 us  [on_device(): pl.pallas_call(functools.partial(outer_kernel, per, nx), grid=(groups, nk...]
    pallas_call x5, Pallas kernels: 54.6 us -> 36.4 us  [inner(): pl.pallas_call(functools.partial(inner_kernel, per, len(carried)), grid=(...]
    ppermute x1 -> x4, waiting for transfers between devices: 0.01 us -> 15.8 us  [the longest x1 11.2 us: carry(): lines = [line] + [lax.ppermute(line, 'ctx', t) for t in turns[1:]]]
    ppermute x2, waiting for transfers between devices: 10.8 us -> 4.27 us  [exchange(): got.append(lax.ppermute(sent, 'ctx', pairs))]
    ppermute x3, waiting for transfers between devices: 3.88 us -> 8.29 us  [carry(): lax.ppermute(down_send, 'ctx', down)]
    ppermute x2, starting transfers between devices: 0.58 us -> 4.43 us  [exchange(): got.append(lax.ppermute(sent, 'ctx', pairs))]
    another operation x2 -> x0, other arithmetic: 3.51 us -> none  [carry(): both = jnp.stack(by_sender(got, nx, x), axis=1)]
  transfers between devices with their start and end apart: 9 -> 12, of which waited for: 4 -> 6; matrix products, arithmetic and copies ran while one was open for 3% -> 3% of each run, Pallas kernels for 37% -> 23%
where the time goes in v2:
time: 162 us; the launch traced here: 160 us
  Pallas kernels  88.9 us (55%)
  waiting for transfers between devices  28.4 us (18%)
  local copies, waits for them, and re-layouts  16.4 us (10%)
  starting transfers between devices  15.6 us (10%)
  other arithmetic  9.79 us (6%)
    pallas_call x5, Pallas kernels, inner(): pl.pallas_call(functools.partial(inner_kernel, per, len(carried)), grid=(...  36.4 us
    pallas_call x1, Pallas kernels, on_device(): pl.pallas_call(functools.partial(outer_kernel, per, nx), grid=(groups, nk...  30.1 us
    pallas_call x1, Pallas kernels, on_device(): pl.pallas_call(functools.partial(state_kernel, per), grid=(groups, nk), i...  20.9 us
    unnamed x43, local copies, waits for them, and re-layouts  11.7 us
    ppermute x1, waiting for transfers between devices, carry(): lines = [line] + [lax.ppermute(line, 'ctx', t) for t in turns[1:]]  11.2 us
    ppermute x3, waiting for transfers between devices, carry(): lax.ppermute(down_send, 'ctx', down)  8.29 us
    ppermute x3, starting transfers between devices, carry(): lax.ppermute(up_send, 'ctx', up)  5.34 us
    ppermute x3, waiting for transfers between devices, carry(): lax.ppermute(skip, 'ctx', [(c * nx + i, (c + r) % nz * nx + i) for c in r...  4.68 us
  transfers between devices with their start and end apart: 12, of which 6 were waited for; matrix products, arithmetic and copies ran while one was open for 3% of the time, Pallas kernels for 23%

profile of v2, /device:TPU:0, one launch (start us, length us, event | category | flops | bytes accessed | tf_op | source)
XLA Modules:
  0.0 160.2 jit_solution(14373851357614835073)
XLA Ops:
  6.2 1.6 %prep.1 = (f32[1024,256]{1,0:T(8,128)S(1)}, f32[96,1024]{1,0:T(8,128)S(1)}) custom-call(f32[32,1024]{1,0:T(8,128)S(1)} %copy-done.14, f32[32,1024]{1,0:T(8,128)S(1)} %copy-done.15), custom_call_target="tpu_custom_call" | custom-call | tf_op jit(solution)/shard_map/prep/pallas_call | solution.py:289
  10.1 20.9 %states.1 = (f32[8,128,2048]{2,1,0:T(8,128)}, f32[8,128,2048]{2,1,0:T(8,128)}, f32[2,128,2048]{2,1,0:T(8,128)S(1)}, f32[1,2048]{1,0:T(1,128)S(1)}) custom-call(bf16[1024,2048]{1,0:T(8,128)(2,1)} %x_ref.13, bf16[1024,2048]{1,0:T(8,128)(2,1)} %dy_ref.13, bf16[1024,256]{1,0:T(8,128)(2,1)S(1)} %copy-done, bf16[1024,256]{1,0:T(8,128)(2,1)S(1)} %copy-done.5, ...), custom_call_target="tpu_custom_call" | custom-call | flops 2147483648 | bytes 25165824 | tf_op jit(solution)/shard_map/states/pallas_call | solution.py:322
  31.0 1.6 dynamic-slice_bitcast_fusion
  32.6 2.9 %collective-permute-start = (f32[2,64,2048]{2,1,0:T(8,128)}, f32[2,64,2048]{2,1,0:T(8,128)}, u32[]{:S(2)}, u32[]{:S(2)}) collective-permute-start(f32[2,64,2048]{2,1,0:T(8,128)} %get-tuple-element.150), channel_id=1, source_target_pairs={{0,4},{4,0},{8,12},{12,8},{16,20},{20,16},{24,28},{28,24},{1,5},{5... | collective-permute-start | bytes 3145736 | tf_op jit(solution)/shard_map/ppermute | solution.py:209
  39.6 8.6 %inner.5 = (f32[1024,2048]{1,0:T(8,128)}, f32[1024,256]{1,0:T(8,128)S(1)}, f32[1024,256]{1,0:T(8,128)S(1)}, f32[64,1024]{1,0:T(8,128)S(1)}) custom-call(bf16[1024,2048]{1,0:T(8,128)(2,1)} %x_ref.13, bf16[1024,2048]{1,0:T(8,128)(2,1)} %dy_ref.13, bf16[1024,256]{1,0:T(8,128)(2,1)S(1)} %copy-done.1, bf16[1024,256]{1,0:T(8,128)(2,1)S(1)} %copy-done.6, ...), custom_call_target="tpu_custom_call" | custom-call | flops 8000000000 | bytes 4194304 | tf_op jit(solution)/shard_map/inner/pallas_call | solution.py:347
  48.2 11.2 %collective-permute-done.1 = f32[2,2048]{1,0:T(2,128)} collective-permute-done((f32[2,2048]{1,0:T(2,128)}, f32[2,2048]{1,0:T(2,128)}, u32[]{:S(2)}, u32[]{:S(2)}) %collective-permute-start.1) | collective-permute-done | bytes 16416 | tf_op jit(solution)/shard_map/ppermute | solution.py:235
  60.1 1.8 %broadcast_select_fusion = (f32[2,64,2048]{2,1,0:T(8,128)S(1)}, f32[2,64,2048]{2,1,0:T(8,128)S(1)}) fusion(f32[2,64,2048]{2,1,0:T(8,128)} %collective-permute-done, f32[2,64,2048]{2,1,0:T(8,128)} %get-tuple-element.86, pred[]{:T(512)S(6)} %eq.64, pred[]{:T(512)S(6)} %eq.65), kind=kLoop, calls=%fused_computation.24 | loop fusion | flops 524288 | bytes 4194306 | tf_op jit(solution)/shard_map/jit(_where)/select_n | solution.py:218
  62.8 3.8 %collective-permute-start.2 = (f32[64,2048]{1,0:T(8,128)S(1)}, f32[64,2048]{1,0:T(8,128)S(1)}, u32[]{:S(2)}, u32[]{:S(2)}) collective-permute-start(f32[64,2048]{1,0:T(8,128)S(1)} %get-tuple-element.147), channel_id=1, source_target_pairs={{0,8},{4,12},{1,9},{5,13},{2,10},{6,14},{3,11},{7,15}} | collective-permute-start | bytes 1572872 | tf_op jit(solution)/shard_map/ppermute | solution.py:259
  66.5 2.5 %collective-permute-start.6 = (f32[1,2048]{1,0:T(1,128)S(1)}, f32[1,2048]{1,0:T(1,128)S(1)}, u32[]{:S(2)}, u32[]{:S(2)}) collective-permute-start(f32[1,2048]{1,0:T(1,128)S(1)} %get-tuple-element.139), channel_id=1, source_target_pairs={{0,24},{4,28},{8,0},{12,4},{16,8},{20,12},{24,16},{28,20},{1,25},{... | collective-permute-start | bytes 24584 | tf_op jit(solution)/shard_map/ppermute | solution.py:246
  69.7 5.1 %inner.6 = (f32[1024,2048]{1,0:T(8,128)}, f32[1024,256]{1,0:T(8,128)S(1)}, f32[1024,256]{1,0:T(8,128)S(1)}, f32[64,1024]{1,0:T(8,128)S(1)}) custom-call(bf16[1024,2048]{1,0:T(8,128)(2,1)} %x_ref.13, bf16[1024,2048]{1,0:T(8,128)(2,1)} %dy_ref.13, ...), custom_call_target="tpu_custom_call", output_to_operand_aliasing={{0}: (6, {}), {1}: (7, {}), {2}: (8, {}), {3}: (9, {})} | custom-call | flops 4000000000 | bytes 2097152 | tf_op jit(solution)/shard_map/inner/pallas_call | solution.py:347
  74.8 2.3 %collective-permute-done.6 = f32[1,2048]{1,0:T(1,128)S(1)} collective-permute-done((f32[1,2048]{1,0:T(1,128)S(1)}, f32[1,2048]{1,0:T(1,128)S(1)}, u32[]{:S(2)}, u32[]{:S(2)}) %collective-permute-start.6) | collective-permute-done | bytes 8224 | tf_op jit(solution)/shard_map/ppermute | solution.py:246
  77.2 2.3 %collective-permute-done.4 = f32[1,2048]{1,0:T(1,128)S(1)} collective-permute-done((f32[1,2048]{1,0:T(1,128)S(1)}, f32[1,2048]{1,0:T(1,128)S(1)}, u32[]{:S(2)}, u32[]{:S(2)}) %collective-permute-start.4) | collective-permute-done | bytes 8224 | tf_op jit(solution)/shard_map/ppermute | solution.py:246
  81.7 8.6 %inner.7 = (f32[1024,2048]{1,0:T(8,128)}, f32[1024,256]{1,0:T(8,128)S(1)}, f32[1024,256]{1,0:T(8,128)S(1)}, f32[64,1024]{1,0:T(8,128)S(1)}) custom-call(bf16[1024,2048]{1,0:T(8,128)(2,1)} %x_ref.13, bf16[1024,2048]{1,0:T(8,128)(2,1)} %dy_ref.13, ...), custom_call_target="tpu_custom_call", output_to_operand_aliasing={{0}: (6, {}), {1}: (7, {}), {2}: (8, {}), {3}: (9, {})} | custom-call | flops 8000000000 | bytes 4194304 | tf_op jit(solution)/shard_map/inner/pallas_call | solution.py:347
  90.7 1.3 collective-permute-start.10
  92.8 5.1 %inner.8 = (f32[1024,2048]{1,0:T(8,128)}, f32[1024,256]{1,0:T(8,128)S(1)}, f32[1024,256]{1,0:T(8,128)S(1)}, f32[64,1024]{1,0:T(8,128)S(1)}) custom-call(bf16[1024,2048]{1,0:T(8,128)(2,1)} %x_ref.13, bf16[1024,2048]{1,0:T(8,128)(2,1)} %dy_ref.13, ...), custom_call_target="tpu_custom_call", output_to_operand_aliasing={{0}: (6, {}), {1}: (7, {}), {2}: (8, {}), {3}: (9, {})} | custom-call | flops 4000000000 | bytes 2097152 | tf_op jit(solution)/shard_map/inner/pallas_call | solution.py:347
  98.0 8.3 %collective-permute-done.10 = f32[64,2048]{1,0:T(8,128)S(1)} collective-permute-done((f32[64,2048]{1,0:T(8,128)S(1)}, f32[64,2048]{1,0:T(8,128)S(1)}, u32[]{:S(2)}, u32[]{:S(2)}) %collective-permute-start.10) | collective-permute-done | bytes 524320 | tf_op jit(solution)/shard_map/ppermute | solution.py:259
  106.7 1.5 fusion.1
  108.2 1.5 collective-permute-start.11
  109.7 1.4 fusion.9
  111.1 1.4 reshape.37
  112.5 1.3 reduce_sum.39
  116.9 8.8 %inner.9 = (f32[1024,2048]{1,0:T(8,128)}, f32[1024,256]{1,0:T(8,128)S(1)}, f32[1024,256]{1,0:T(8,128)S(1)}, f32[64,1024]{1,0:T(8,128)S(1)}) custom-call(bf16[1024,2048]{1,0:T(8,128)(2,1)} %x_ref.13, bf16[1024,2048]{1,0:T(8,128)(2,1)} %dy_ref.13, ...), custom_call_target="tpu_custom_call", output_to_operand_aliasing={{0}: (6, {}), {1}: (7, {}), {2}: (8, {}), {3}: (9, {})} | custom-call | flops 8000000000 | bytes 4194304 | tf_op jit(solution)/shard_map/inner/pallas_call | solution.py:347
  125.7 4.3 %collective-permute-done.11.rest_1_ = f32[2,64,2048]{2,1,0:T(8,128)} collective-permute-done((f32[2,64,2048]{2,1,0:T(8,128)}, f32[2,64,2048]{2,1,0:T(8,128)}, u32[]{:S(2)}, u32[]{:S(2)}) %collective-permute-start.11) | collective-permute-done | bytes 1048608 | tf_op jit(solution)/shard_map/ppermute | solution.py:209
  130.0 30.1 %outer.1 = (bf16[1024,2048]{1,0:T(8,128)(2,1)}, f32[32,1024]{1,0:T(8,128)}, f32[32,1024]{1,0:T(8,128)}, bf16[1024,256]{1,0:T(8,128)(2,1)}, bf16[1024,256]{1,0:T(8,128)(2,1)}) custom-call(bf16[1024,2048]{1,0:T(8,128)(2,1)} %x_ref.13, bf16[1024,2048]{1,0:T(8,128)(2,1)} %dy_ref.13, bf16[1024,256]{1,0:T(8,128)(2,1)S(1)} %copy-done.4, ...), custom_call_target="tpu_custom_call" | custom-call | flops 4294967296 | bytes 41943040 | tf_op jit(solution)/shard_map/outer/pallas_call | solution.py:384
  (82 shorter events, 20.9 us)
Async XLA Ops:
  7.8 23.1 %copy-start.10 = (f32[96,1024]{1,0:T(8,128)}, f32[96,1024]{1,0:T(8,128)S(1)}, u32[]{:S(2)}) copy-start(f32[96,1024]{1,0:T(8,128)S(1)} %get-tuple-element.74.row_ref) | copy-start | bytes 1179652
  7.9 1.2 copy-start
  9.0 1.0 copy-start.5
  32.6 26.8 %collective-permute-start = (f32[2,64,2048]{2,1,0:T(8,128)}, f32[2,64,2048]{2,1,0:T(8,128)}, u32[]{:S(2)}, u32[]{:S(2)}) collective-permute-start(f32[2,64,2048]{2,1,0:T(8,128)} %get-tuple-element.150), channel_id=1, source_target_pairs={{0,4},{4,0},{8,12},{12,8},{16,20},{20,16},{24,28},{28,24},{1,5},{5... | collective-permute-start | bytes 3145736 | tf_op jit(solution)/shard_map/ppermute | solution.py:209
  36.5 22.9 %collective-permute-start.1 = (f32[2,2048]{1,0:T(2,128)}, f32[2,2048]{1,0:T(2,128)}, u32[]{:S(2)}, u32[]{:S(2)}) collective-permute-start(f32[2,2048]{1,0:T(2,128)} %pad_maximum_fusion.1), channel_id=1, source_target_pairs={{0,4},{4,0},{8,12},{12,8},{16,20},{20,16},{24,28},{28,24},{1,5},{5... | collective-permute-start | bytes 49160 | tf_op jit(solution)/shard_map/ppermute | solution.py:235
  48.2 21.5 %copy-start.2 = (bf16[1024,256]{1,0:T(8,128)(2,1)S(1)}, bf16[1024,256]{1,0:T(8,128)(2,1)}, u32[]{:S(2)}) copy-start(bf16[1024,256]{1,0:T(8,128)(2,1)} %k_ref.13) | copy-start | bytes 1572868
  48.2 21.5 %copy-start.7 = (bf16[1024,256]{1,0:T(8,128)(2,1)S(1)}, bf16[1024,256]{1,0:T(8,128)(2,1)}, u32[]{:S(2)}) copy-start(bf16[1024,256]{1,0:T(8,128)(2,1)} %q_ref.13) | copy-start | bytes 1572868
  48.2 21.5 %copy-start.12 = (f32[96,1024]{1,0:T(8,128)S(1)}, f32[96,1024]{1,0:T(8,128)}, u32[]{:S(2)}) copy-start(f32[96,1024]{1,0:T(8,128)} %copy-done.10) | copy-start | bytes 1179652
  61.9 12.9 %copy-start.17 = (f32[1,2048]{1,0:T(1,128)}, f32[1,2048]{1,0:T(1,128)S(1)}, u32[]{:S(2)}) copy-start(f32[1,2048]{1,0:T(1,128)S(1)} %get-tuple-element.139) | copy-start | bytes 24580
  62.1 17.5 %collective-permute-start.3 = (f32[64,2048]{1,0:T(8,128)S(1)}, f32[64,2048]{1,0:T(8,128)S(1)}, u32[]{:S(2)}, u32[]{:S(2)}) collective-permute-start(f32[64,2048]{1,0:T(8,128)S(1)} %get-tuple-element.146), channel_id=1, source_target_pairs={{24,16},{28,20},{25,17},{29,21},{26,18},{30,22},{27,19},{31,23}} | collective-permute-start | bytes 1572872 | tf_op jit(solution)/shard_map/ppermute | solution.py:259
  62.8 16.8 %collective-permute-start.2 = (f32[64,2048]{1,0:T(8,128)S(1)}, f32[64,2048]{1,0:T(8,128)S(1)}, u32[]{:S(2)}, u32[]{:S(2)}) collective-permute-start(f32[64,2048]{1,0:T(8,128)S(1)} %get-tuple-element.147), channel_id=1, source_target_pairs={{0,8},{4,12},{1,9},{5,13},{2,10},{6,14},{3,11},{7,15}} | collective-permute-start | bytes 1572872 | tf_op jit(solution)/shard_map/ppermute | solution.py:259
  66.5 10.6 %collective-permute-start.6 = (f32[1,2048]{1,0:T(1,128)S(1)}, f32[1,2048]{1,0:T(1,128)S(1)}, u32[]{:S(2)}, u32[]{:S(2)}) collective-permute-start(f32[1,2048]{1,0:T(1,128)S(1)} %get-tuple-element.139), channel_id=1, source_target_pairs={{0,24},{4,28},{8,0},{12,4},{16,8},{20,12},{24,16},{28,20},{1,25},{... | collective-permute-start | bytes 24584 | tf_op jit(solution)/shard_map/ppermute | solution.py:246
  69.1 8.2 %collective-permute-start.5 = (f32[1,2048]{1,0:T(1,128)S(1)}, f32[1,2048]{1,0:T(1,128)S(1)}, u32[]{:S(2)}, u32[]{:S(2)}) collective-permute-start(f32[1,2048]{1,0:T(1,128)S(1)} %get-tuple-element.139), channel_id=1, source_target_pairs={{0,16},{4,20},{8,24},{12,28},{16,0},{20,4},{24,8},{28,12},{1,17},{... | collective-permute-start | bytes 24584 | tf_op jit(solution)/shard_map/ppermute | solution.py:246
  69.1 10.5 %collective-permute-start.4 = (f32[1,2048]{1,0:T(1,128)S(1)}, f32[1,2048]{1,0:T(1,128)S(1)}, u32[]{:S(2)}, u32[]{:S(2)}) collective-permute-start(f32[1,2048]{1,0:T(1,128)S(1)} %get-tuple-element.139), channel_id=1, source_target_pairs={{0,8},{4,12},{8,16},{12,20},{16,24},{20,28},{24,0},{28,4},{1,9},{5... | collective-permute-start | bytes 24584 | tf_op jit(solution)/shard_map/ppermute | solution.py:246
  77.1 2.4 %copy-start.18 = (f32[1,2048]{1,0:T(1,128)}, f32[1,2048]{1,0:T(1,128)S(1)}, u32[]{:S(2)}) copy-start(f32[1,2048]{1,0:T(1,128)S(1)} %collective-permute-done.6) | copy-start | bytes 24580
  77.2 2.3 %copy-start.19 = (f32[1,2048]{1,0:T(1,128)}, f32[1,2048]{1,0:T(1,128)S(1)}, u32[]{:S(2)}) copy-start(f32[1,2048]{1,0:T(1,128)S(1)} %collective-permute-done.5) | copy-start | bytes 24580
  80.3 10.0 %collective-permute-start.8 = (f32[64,2048]{1,0:T(8,128)S(1)}, f32[64,2048]{1,0:T(8,128)S(1)}, u32[]{:S(2)}, u32[]{:S(2)}) collective-permute-start(f32[64,2048]{1,0:T(8,128)S(1)} %get-tuple-element.164), channel_id=1, source_target_pairs={{16,8},{20,12},{17,9},{21,13},{18,10},{22,14},{19,11},{23,15}} | collective-permute-start | bytes 1572872 | tf_op jit(solution)/shard_map/ppermute | solution.py:259
  81.0 9.3 %collective-permute-start.7 = (f32[64,2048]{1,0:T(8,128)S(1)}, f32[64,2048]{1,0:T(8,128)S(1)}, u32[]{:S(2)}, u32[]{:S(2)}) collective-permute-start(f32[64,2048]{1,0:T(8,128)S(1)} %get-tuple-element.165), channel_id=1, source_target_pairs={{8,16},{12,20},{9,17},{13,21},{10,18},{14,22},{11,19},{15,23}} | collective-permute-start | bytes 1572872 | tf_op jit(solution)/shard_map/ppermute | solution.py:259
  90.7 15.6 %collective-permute-start.10 = (f32[64,2048]{1,0:T(8,128)S(1)}, f32[64,2048]{1,0:T(8,128)S(1)}, u32[]{:S(2)}, u32[]{:S(2)}) collective-permute-start(f32[64,2048]{1,0:T(8,128)S(1)} %get-tuple-element.140), channel_id=1, source_target_pairs={{8,0},{12,4},{9,1},{13,5},{10,2},{14,6},{11,3},{15,7}} | collective-permute-start | bytes 1572872 | tf_op jit(solution)/shard_map/ppermute | solution.py:259
  92.0 14.3 %collective-permute-start.9 = (f32[64,2048]{1,0:T(8,128)S(1)}, f32[64,2048]{1,0:T(8,128)S(1)}, u32[]{:S(2)}, u32[]{:S(2)}) collective-permute-start(f32[64,2048]{1,0:T(8,128)S(1)} %get-tuple-element.162), channel_id=1, source_target_pairs={{16,24},{20,28},{17,25},{21,29},{18,26},{22,30},{19,27},{23,31}} | collective-permute-start | bytes 1572872 | tf_op jit(solution)/shard_map/ppermute | solution.py:259
  108.2 21.8 %collective-permute-start.11 = (f32[2,64,2048]{2,1,0:T(8,128)}, f32[2,64,2048]{2,1,0:T(8,128)}, u32[]{:S(2)}, u32[]{:S(2)}) collective-permute-start(f32[2,64,2048]{2,1,0:T(8,128)} %get-tuple-element.144), channel_id=1, source_target_pairs={{0,4},{4,0},{8,12},{12,8},{16,20},{20,16},{24,28},{28,24},{1,5},{5... | collective-permute-start | bytes 3145736 | tf_op jit(solution)/shard_map/ppermute | solution.py:209
  116.9 13.1 %copy-start.4 = (bf16[1024,256]{1,0:T(8,128)(2,1)S(1)}, bf16[1024,256]{1,0:T(8,128)(2,1)}, u32[]{:S(2)}) copy-start(bf16[1024,256]{1,0:T(8,128)(2,1)} %k_ref.13) | copy-start | bytes 1572868
  116.9 13.1 %copy-start.9 = (f32[2,64,2048]{2,1,0:T(8,128)S(1)}, f32[2,64,2048]{2,1,0:T(8,128)}, u32[]{:S(2)}) copy-start(f32[2,64,2048]{2,1,0:T(8,128)} %get-tuple-element.129.rest_0_) | copy-start | bytes 3145732
  116.9 13.1 %copy-start.16 = (f32[32,1024]{1,0:T(8,128)S(1)}, f32[32,1024]{1,0:T(8,128)}, u32[]{:S(2)}) copy-start(f32[32,1024]{1,0:T(8,128)} %step_ref.3) | copy-start | bytes 393220
  (9 other events, 8.6 us)

commit v3 on v2

--- a/solution.py
+++ b/solution.py
@@ -10,6 +10,7 @@
 P_SIZE = 64
 N = 128
 C = 128
+INNER_MARKS = {False: (0.25, 0.4, 0.6, 0.75, 1.0), True: (0.375, 0.5, 0.625, 1.0)}
 LOG2E = 1.4426950408889634
 F32 = jnp.float32
 BF16 = jnp.bfloat16
@@ -69,7 +70,7 @@
 
 def state_kernel(per, x_ref, dy_ref, k_ref, q_ref, col_ref, tot_ref, pre_ref,
                  h_ref, u_ref, ends_ref, skip_ref, h_s, g_s):
-    k = pl.program_id(1)
+    k = pl.program_id(0)
 
     @pl.when(k == 0)
     def _():
@@ -98,7 +99,7 @@
     both = x_ref[...].astype(F32) * dy_ref[...].astype(F32)
     skip_ref[...] = skip_ref[...] + jnp.sum(both, axis=0, keepdims=True)
 
-    @pl.when(k == pl.num_programs(1) - 1)
+    @pl.when(k == pl.num_programs(0) - 1)
     def _():
         ends_ref[0] = h_s[...]
         ends_ref[1] = g_s[...]
@@ -137,13 +138,13 @@
     rc_ref[per:, :] = c_s[...].T[:per]
 
 
-def outer_kernel(per, nx, x_ref, dy_ref, k_ref, q_ref, col_ref, row_ref, step_ref, h_ref, u_ref,
+def outer_kernel(per, nx, carried, x_ref, dy_ref, k_ref, q_ref, col_ref, row_ref, step_ref, h_ref, u_ref,
                  tot_ref, pre_ref, gain_ref, z_ref, gq_ref, gk_ref, rc_ref, *rest):
     got = rest[:nx]
-    gx_ref, gstep_ref, gdecay_ref, gkey_ref, gquery_ref, e_s, g_s, r_s, c_s, edge_s = rest[nx:]
+    gx_ref, gstep_ref, gdecay_ref, gkey_ref, gquery_ref, e_s, g_s, r_s, c_s, edge_s = rest[nx + carried :]
     place = lax.rem(lax.axis_index("ctx"), nx)
 
-    @pl.when(pl.program_id(1) == 0)
+    @pl.when(pl.program_id(0) == 0)
     def _():
         size = N // nx
         for r in range(nx):
@@ -220,30 +221,11 @@
     return out
 
 
-def held(value, work):
-    return lax.optimization_barrier((value, work))
-
-
-def carry(ends, fade, skip, stages, work):
-    count = lax.axis_size("ctx")
-    nx = 2 if count < 16 else 4
-    nz = count // nx
-    place = lax.axis_index("ctx")
-    x, z = place % nx, place // nx
-    turns = [[(c * nx + i, c * nx + (i + r) % nx) for c in range(nz) for i in range(nx)] for r in range(nx)]
-    line = jnp.concatenate([fade, skip], axis=0)
-    lines = [line] + [lax.ppermute(line, "ctx", t) for t in turns[1:]]
-    _, rows, width = ends.shape
-    got = exchange(ends.reshape(2, nx, rows // nx, width), nx, x, nz)
-    work = stages[0](work)
-    (got, lines), work = held((got, lines), work)
-    lines = by_sender(lines, nx, x)
-    row_fade = [one[:1] for one in lines]
+def carry_steps(ends, fades, nx, nz, x):
+    _, rows, wide = ends.shape
+    got = yield exchange(ends.reshape(2, nx, rows // nx, wide), nx, x, nz)
+    row_fade = fades()
     all_fade = functools.reduce(lambda a, b: a * b, row_fade)
-    skip = functools.reduce(lambda a, b: a + b, [one[1:] for one in lines])
-    skips = [skip]
-    for r in range(1, nz):
-        skips.append(lax.ppermute(skip, "ctx", [(c * nx + i, (c + r) % nz * nx + i) for c in range(nz) for i in range(nx)]))
     both = by_sender(got, nx, x)
     states, pulls = [b[0] for b in both], [b[1] for b in both]
     state_sum = states[0]
@@ -256,13 +238,7 @@
     for hop in range(nz - 1):
         up = [(hop * nx + i, (hop + 1) * nx + i) for i in range(nx)]
         down = [((nz - 1 - hop) * nx + i, (nz - 2 - hop) * nx + i) for i in range(nx)]
-        came = (lax.ppermute(up_send, "ctx", up), lax.ppermute(down_send, "ctx", down))
-        work = stages[1 + hop](work)
-        if hop == 0:
-            (came, skips), work = held((came, skips), work)
-            skip = functools.reduce(lambda a, b: a + b, by_sender(skips, nz, z))
-        else:
-            came, work = held(came, work)
+        came = yield (lax.ppermute(up_send, "ctx", up), lax.ppermute(down_send, "ctx", down))
         entering = came[0] if hop == 0 else entering + came[0]
         leaving = came[1] if hop == 0 else leaving + came[1]
         up_send = all_fade * entering + state_sum
@@ -272,10 +248,7 @@
         ins.append(row_fade[i] * ins[-1] + states[i])
     for i in range(nx - 1, 0, -1):
         outs.append(row_fade[i] * outs[-1] + pulls[i])
-    got = exchange(jnp.stack([jnp.stack(ins), jnp.stack(outs[::-1])]), nx, x, nz)
-    work = stages[nz](work)
-    got, work = held(got, work)
-    return got, skip, work
+    yield exchange(jnp.stack([jnp.stack(ins), jnp.stack(outs[::-1])]), nx, x, nz)
 
 
 def on_device(signal, step_size, log_decay, input_map, output_map, skip_gain, grad_out):
@@ -312,29 +285,37 @@
         return (
             spec((C, wide), lambda g, k: (at(k), g)),
             spec((C, C), lambda g, k: (at(k), g)),
-            spec((1, N, wide), lambda g, k: (at(k), 0, g)),
-            spec((1, 1, wide), lambda g, k: (at(k), 0, g)),
-            spec((1, 1, wide), lambda g, k: (nk + at(k), 0, g)),
         )
 
-    big, small, local, tot, pre = specs(lambda k: k)
-
-    states, pulls, ends, skip = pl.pallas_call(
-        functools.partial(state_kernel, per),
-        grid=(groups, nk),
-        in_specs=[big, big, small, small, small, tot, pre],
-        out_specs=(local, local, spec((2, N, wide), lambda g, k: (0, 0, g)), spec((1, wide), lambda g, k: (0, g))),
-        out_shape=(
-            jax.ShapeDtypeStruct((nk, N, width), F32),
-            jax.ShapeDtypeStruct((nk, N, width), F32),
-            jax.ShapeDtypeStruct((2, N, width), F32),
-            jax.ShapeDtypeStruct((1, width), F32),
-        ),
-        scratch_shapes=[pltpu.VMEM((N, wide), F32), pltpu.VMEM((N, wide), F32)],
-        compiler_params=params(),
-        cost_estimate=pl.CostEstimate(flops=8 * length * width * N, bytes_accessed=24 << 20, transcendentals=0),
-        name="states",
-    )(signal, grad_out, input_map, output_map, col, lines, lines)
+    def fixed(at, g):
+        return (
+            spec((C, wide), lambda k: (at(k), g)),
+            spec((C, C), lambda k: (at(k), g)),
+            spec((1, N, wide), lambda k: (at(k), 0, 0)),
+            spec((1, 1, wide), lambda k: (at(k), 0, g)),
+            spec((1, 1, wide), lambda k: (nk + at(k), 0, g)),
+        )
+
+    def state_call(g, row):
+        big, small, local, tot, pre = fixed(lambda k: k, g)
+        return pl.pallas_call(
+            functools.partial(state_kernel, per),
+            grid=(nk,),
+            in_specs=[big, big, small, small, small, tot, pre],
+            out_specs=(local, local, spec((2, N, wide), lambda k: (0, 0, 0)), spec((1, wide), lambda k: (0, 0))),
+            out_shape=(
+                jax.ShapeDtypeStruct((nk, N, wide), F32),
+                jax.ShapeDtypeStruct((nk, N, wide), F32),
+                jax.ShapeDtypeStruct((2, N, wide), F32),
+                jax.ShapeDtypeStruct((1, wide), F32),
+            ),
+            scratch_shapes=[pltpu.VMEM((N, wide), F32), pltpu.VMEM((N, wide), F32)],
+            compiler_params=params(),
+            cost_estimate=pl.CostEstimate(
+                flops=8 * length * wide * N, bytes_accessed=12 << 20, transcendentals=0
+            ),
+            name="states",
+        )(signal, grad_out, input_map, output_map, col, lines, lines)
 
     inner_shapes = (
         jax.ShapeDtypeStruct((length, width), F32),
@@ -342,8 +323,8 @@
         jax.ShapeDtypeStruct((length, groups * N), F32),
         jax.ShapeDtypeStruct((2 * heads, length), F32),
     )
-    def inner(first, each, carried):
-        b, s, _, _, _ = specs(lambda k: first + k)
+    def inner(first, each, carried, row):
+        b, s = specs(lambda k: first + k)
         return pl.pallas_call(
             functools.partial(inner_kernel, per, len(carried)),
             grid=(groups, each),
@@ -360,55 +341,102 @@
             name="inner",
         )(signal, grad_out, input_map, output_map, col, row, *carried)
 
+    def outer(g, sums_in, got, work, results):
+        def back(k):
+            return nk - 1 - k
+
+        big, small, local, tot, pre = fixed(back, g)
+        rowed = spec((per, C), lambda k: (g, back(k)))
+        operands = [signal, grad_out, input_map, output_map, col, row, step_size, *sums_in,
+                    lines, lines, lines, *work, *got]
+        return pl.pallas_call(
+            functools.partial(outer_kernel, per, nx, len(results)),
+            grid=(nk,),
+            in_specs=[big, big, small, small, small, spec((3 * per, C), lambda k: (g, back(k))), rowed,
+                      local, local, tot, pre, spec((1, 1, wide), lambda k: (2 * nk + 1, 0, g)),
+                      big, small, small, spec((2 * per, C), lambda k: (g, back(k)))]
+            + [spec((2, N // nx, wide), lambda k: (0, 0, 0))] * nx
+            + [pl.BlockSpec(memory_space=pltpu.HBM)] * len(results),
+            out_specs=(big, rowed, rowed, small, small),
+            out_shape=(
+                jax.ShapeDtypeStruct((length, width), BF16),
+                jax.ShapeDtypeStruct((heads, length), F32),
+                jax.ShapeDtypeStruct((heads, length), F32),
+                jax.ShapeDtypeStruct((length, groups * N), BF16),
+                jax.ShapeDtypeStruct((length, groups * N), BF16),
+            ),
+            scratch_shapes=[
+                pltpu.VMEM((N, wide), F32),
+                pltpu.VMEM((N, wide), F32),
+                pltpu.VMEM((per, C), F32),
+                pltpu.VMEM((per, C), F32),
+                pltpu.VMEM((per, C), F32),
+            ],
+            input_output_aliases={len(operands) + i: i for i in range(len(results))},
+            compiler_params=params(),
+            cost_estimate=pl.CostEstimate(
+                flops=16 * length * wide * N, bytes_accessed=20 << 20, transcendentals=0
+            ),
+            name="outer",
+        )(*operands, *results)
+
     count = lax.axis_size("ctx")
-    hops = count // (2 if count < 16 else 4) + 1
-    marks = [round(i * nk / hops) for i in range(hops + 1)]
-
-    def stage(i):
-        def run(carried):
-            first, each = marks[i], marks[i + 1] - marks[i]
-            return inner(first, each, carried) if each else carried
-
-        return run
-
-    got, skip, carried = carry(ends, fade, skip, [stage(i) for i in range(hops)], ())
-    z, gq, gk, rc = carried
-    nx = len(got)
+    nx = 2 if count < 16 else 4
+    nz = count // nx
+    place = lax.axis_index("ctx")
+    x = place % nx
+    marks = [0] + [max(1, round(nk * f)) for f in INNER_MARKS[groups > 1]]
+    local, sections, arrived = {}, {}, {}
+    skip, strides = None, [1 << i for i in range(count.bit_length() - 1)]
+    fades = [fade] + [
+        lax.ppermute(fade, "ctx", [(c * nx + i, c * nx + (i + r) % nx) for c in range(nz) for i in range(nx)])
+        for r in range(1, nx)
+    ]
+    fade_rows = []
+    work, results = (), ()
+    local[0] = state_call(0, row)
+    for tick in range(nz + groups + 1):
+        sent = {}
+        for g in range(groups):
+            if tick == g:
+                def faded(g=g):
+                    return [f[:, g * wide : (g + 1) * wide] for f in fade_rows]
+
+                sections[g] = carry_steps(local[g][2], faded, nx, nz, x)
+                sent[g] = next(sections[g])
+            elif g < tick <= g + nz:
+                sent[g] = sections[g].send(arrived[g])
+        moved_skip = ()
+        if skip is None and len(local) == groups:
+            skip = jnp.concatenate([local[g][3] for g in range(groups)], axis=1)
+        if skip is not None and strides:
+            stride = strides.pop(0)
+            moved_skip = lax.ppermute(skip, "ctx", [(i, i ^ stride) for i in range(count)])
+        made = None
+        if tick + 1 < groups:
+            made = state_call(tick + 1, row)
+        elif tick <= nz:
+            at = tick - groups + 1
+            if marks[at + 1] > marks[at]:
+                work = inner(marks[at], marks[at + 1] - marks[at], work, row)
+        else:
+            g = tick - nz - 1
+            results = outer(g, local[g][:2], arrived[g], work, results)
+        if tick == nz + groups:
+            break
+        now_fades = fades if tick == 0 else ()
+        sent, moved_skip, made, work, results, row, now_fades = lax.optimization_barrier(
+            (sent, moved_skip, made, work, results, row, now_fades)
+        )
+        arrived.update(sent)
+        if tick == 0:
+            fade_rows.extend(by_sender(now_fades, nx, x))
+        if made is not None:
+            local[tick + 1] = made
+        if not isinstance(moved_skip, tuple):
+            skip = skip + moved_skip
     grad_skip = jnp.sum(skip.reshape(heads, P_SIZE), axis=1)
-
-    def back(k):
-        return nk - 1 - k
-
-    big, small, local, tot, pre = specs(back)
-    rowed = spec((per, C), lambda g, k: (g, back(k)))
-    grad_signal, grad_step, grad_decay, grad_input, grad_output = pl.pallas_call(
-        functools.partial(outer_kernel, per, nx),
-        grid=(groups, nk),
-        in_specs=[big, big, small, small, small, spec((3 * per, C), lambda g, k: (g, back(k))), rowed,
-                  local, local, tot, pre, spec((1, 1, wide), lambda g, k: (2 * nk + 1, 0, g)),
-                  big, small, small, spec((2 * per, C), lambda g, k: (g, back(k)))]
-        + [spec((2, N // nx, wide), lambda g, k: (0, 0, g))] * nx,
-        out_specs=(big, rowed, rowed, small, small),
-        out_shape=(
-            jax.ShapeDtypeStruct((length, width), BF16),
-            jax.ShapeDtypeStruct((heads, length), F32),
-            jax.ShapeDtypeStruct((heads, length), F32),
-            jax.ShapeDtypeStruct((length, groups * N), BF16),
-            jax.ShapeDtypeStruct((length, groups * N), BF16),
-        ),
-        scratch_shapes=[
-            pltpu.VMEM((N, wide), F32),
-            pltpu.VMEM((N, wide), F32),
-            pltpu.VMEM((per, C), F32),
-            pltpu.VMEM((per, C), F32),
-            pltpu.VMEM((per, C), F32),
-        ],
-        compiler_params=params(),
-        cost_estimate=pl.CostEstimate(flops=16 * length * width * N, bytes_accessed=40 << 20, transcendentals=0),
-        name="outer",
-    )(signal, grad_out, input_map, output_map, col, row, step_size, states, pulls,
-      lines, lines, lines, z, gq, gk, rc, *got)
-    return (grad_signal, grad_step, grad_decay, grad_input, grad_output, grad_skip)
+    return (*results, grad_skip)
 
 
 def solution(mesh):

time: 162 us -> 152 us (0.938)
  the two profiles are of different devices: /device:TPU:0 before, /device:TPU:8 now
where the time goes in v3:
time: 152 us; the launch traced here: 151 us
  Pallas kernels  90 us (59%)
  starting transfers between devices  32.1 us (21%)
  local copies, waits for them, and re-layouts  19 us (12%)
  other arithmetic  8.47 us (6%)
    pallas_call x4, Pallas kernels, inner(): pl.pallas_call(functools.partial(inner_kernel, per, len(carried)), grid=(...  34.5 us
    pallas_call x2, Pallas kernels, outer(): pl.pallas_call(functools.partial(outer_kernel, per, nx, len(results)), gr...  31.3 us
    pallas_call x2, Pallas kernels, state_call(): pl.pallas_call(functools.partial(state_kernel, per), grid=(nk,), in_specs...  22.6 us
    unnamed x34, local copies, waits for them, and re-layouts  14.1 us
    ppermute x6, starting transfers between devices, carry_steps(): lax.ppermute(up_send, 'ctx', up)  13.3 us
    ppermute x6, starting transfers between devices, carry_steps(): lax.ppermute(down_send, 'ctx', down)  9.85 us
    ppermute x3, starting transfers between devices, on_device(): lax.ppermute(skip, 'ctx', [(i, i ^ stride) for i in range(count)])  4.28 us
    ppermute x4, starting transfers between devices, exchange(): got.append(lax.ppermute(sent, 'ctx', pairs))  4.12 us
  transfers between devices with their start and end apart: 20, of which 0 were waited for; matrix products, arithmetic and copies ran while one was open for 5% of the time, Pallas kernels for 41%

profile of v3, /device:TPU:8, one launch (start us, length us, event | category | flops | bytes accessed | tf_op | source)
XLA Modules:
  0.0 150.9 jit_solution(13725128670939465602)
XLA Ops:
  6.2 1.6 %prep.1 = (f32[1024,256]{1,0:T(8,128)S(1)}, f32[96,1024]{1,0:T(8,128)S(1)}) custom-call(f32[32,1024]{1,0:T(8,128)S(1)} %copy-done.13, f32[32,1024]{1,0:T(8,128)S(1)} %copy-done.11), custom_call_target="tpu_custom_call" | custom-call | tf_op jit(solution)/shard_map/prep/pallas_call | solution.py:262
  10.7 11.4 %states.2 = (f32[8,128,1024]{2,1,0:T(8,128)}, f32[8,128,1024]{2,1,0:T(8,128)}, f32[2,128,1024]{2,1,0:T(8,128)S(1)}, f32[1,1024]{1,0:T(1,128)S(1)}) custom-call(bf16[1024,2048]{1,0:T(8,128)(2,1)} %x_ref.15, bf16[1024,2048]{1,0:T(8,128)(2,1)} %dy_ref.15, bf16[1024,256]{1,0:T(8,128)(2,1)S(1)} %copy-done, bf16[1024,256]{1,0:T(8,128)(2,1)S(1)} %copy-done.2, ...), custom_call_target="tpu_custom_call" | custom-call | flops 1073741824 | bytes 12582912 | tf_op jit(solution)/shard_map/states/pallas_call | solution.py:301
  23.1 1.5 collective-permute-start
  26.1 11.3 %states.3 = (f32[8,128,1024]{2,1,0:T(8,128)}, f32[8,128,1024]{2,1,0:T(8,128)}, f32[2,128,1024]{2,1,0:T(8,128)S(1)}, f32[1,1024]{1,0:T(1,128)S(1)}) custom-call(bf16[1024,2048]{1,0:T(8,128)(2,1)} %x_ref.15, bf16[1024,2048]{1,0:T(8,128)(2,1)} %dy_ref.15, bf16[1024,256]{1,0:T(8,128)(2,1)S(1)} %copy-done.1, bf16[1024,256]{1,0:T(8,128)(2,1)S(1)} %copy-done.3, ...), custom_call_target="tpu_custom_call" | custom-call | flops 1073741824 | bytes 12582912 | tf_op jit(solution)/shard_map/states/pallas_call | solution.py:301
  38.0 1.5 collective-permute-start.5
  39.5 1.3 broadcast_select_fusion.3
  41.5 1.3 collective-permute-start.2
  44.5 12.1 %inner.4 = (f32[1024,2048]{1,0:T(8,128)}, f32[1024,256]{1,0:T(8,128)S(1)}, f32[1024,256]{1,0:T(8,128)S(1)}, f32[64,1024]{1,0:T(8,128)S(1)}) custom-call(bf16[1024,2048]{1,0:T(8,128)(2,1)} %x_ref.15, bf16[1024,2048]{1,0:T(8,128)(2,1)} %dy_ref.15, bf16[1024,256]{1,0:T(8,128)(2,1)S(1)} %copy-done.1, bf16[1024,256]{1,0:T(8,128)(2,1)S(1)} %copy-done.3, ...), custom_call_target="tpu_custom_call" | custom-call | flops 12000000000 | bytes 6291456 | tf_op jit(solution)/shard_map/inner/pallas_call | solution.py:328
  57.4 2.7 %collective-permute-start.10 = (f32[1,2048]{1,0:T(1,128)S(1)}, f32[1,2048]{1,0:T(1,128)S(1)}, u32[]{:S(2)}, u32[]{:S(2)}) collective-permute-start(f32[1,2048]{1,0:T(1,128)S(1)} %add.134), channel_id=1, source_target_pairs={{0,8},{4,12},{8,0},{12,4},{16,24},{20,28},{24,16},{28,20},{1,9},{5... | collective-permute-start | bytes 24584 | tf_op jit(solution)/shard_map/ppermute | solution.py:414
  60.9 1.3 collective-permute-start.8
  62.3 1.3 collective-permute-start.7
  63.6 4.6 %collective-permute-start.6 = (f32[64,1024]{1,0:T(8,128)S(1)}, f32[64,1024]{1,0:T(8,128)S(1)}, u32[]{:S(2)}, u32[]{:S(2)}) collective-permute-start(f32[64,1024]{1,0:T(8,128)S(1)} %get-tuple-element.245), channel_id=1, source_target_pairs={{8,16},{12,20},{9,17},{13,21},{10,18},{14,22},{11,19},{15,23}} | collective-permute-start | bytes 786440 | tf_op jit(solution)/shard_map/ppermute | solution.py:241
  68.2 5.1 %inner.5 = (f32[1024,2048]{1,0:T(8,128)}, f32[1024,256]{1,0:T(8,128)S(1)}, f32[1024,256]{1,0:T(8,128)S(1)}, f32[64,1024]{1,0:T(8,128)S(1)}) custom-call(bf16[1024,2048]{1,0:T(8,128)(2,1)} %x_ref.15, bf16[1024,2048]{1,0:T(8,128)(2,1)} %dy_ref.15, ...), custom_call_target="tpu_custom_call", output_to_operand_aliasing={{0}: (6, {}), {1}: (7, {}), {2}: (8, {}), {3}: (9, {})} | custom-call | flops 4000000000 | bytes 2097152 | tf_op jit(solution)/shard_map/inner/pallas_call | solution.py:328
  73.6 4.6 %collective-permute-start.12 = (f32[64,1024]{1,0:T(8,128)S(1)}, f32[64,1024]{1,0:T(8,128)S(1)}, u32[]{:S(2)}, u32[]{:S(2)}) collective-permute-start(f32[64,1024]{1,0:T(8,128)S(1)} %get-tuple-element.202), channel_id=1, source_target_pairs={{8,0},{12,4},{9,1},{13,5},{10,2},{14,6},{11,3},{15,7}} | collective-permute-start | bytes 786440 | tf_op jit(solution)/shard_map/ppermute | solution.py:241
  79.0 1.3 collective-permute-start.14
  80.3 4.6 %collective-permute-start.13 = (f32[64,1024]{1,0:T(8,128)S(1)}, f32[64,1024]{1,0:T(8,128)S(1)}, u32[]{:S(2)}, u32[]{:S(2)}) collective-permute-start(f32[64,1024]{1,0:T(8,128)S(1)} %get-tuple-element.241), channel_id=1, source_target_pairs={{8,16},{12,20},{9,17},{13,21},{10,18},{14,22},{11,19},{15,23}} | collective-permute-start | bytes 786440 | tf_op jit(solution)/shard_map/ppermute | solution.py:241
  84.9 5.1 %inner.6 = (f32[1024,2048]{1,0:T(8,128)}, f32[1024,256]{1,0:T(8,128)S(1)}, f32[1024,256]{1,0:T(8,128)S(1)}, f32[64,1024]{1,0:T(8,128)S(1)}) custom-call(bf16[1024,2048]{1,0:T(8,128)(2,1)} %x_ref.15, bf16[1024,2048]{1,0:T(8,128)(2,1)} %dy_ref.15, ...), custom_call_target="tpu_custom_call", output_to_operand_aliasing={{0}: (6, {}), {1}: (7, {}), {2}: (8, {}), {3}: (9, {})} | custom-call | flops 4000000000 | bytes 2097152 | tf_op jit(solution)/shard_map/inner/pallas_call | solution.py:328
  90.2 1.3 collective-permute-start.18
  93.6 1.5 collective-permute-start.16
  95.0 12.2 %inner.7 = (f32[1024,2048]{1,0:T(8,128)}, f32[1024,256]{1,0:T(8,128)S(1)}, f32[1024,256]{1,0:T(8,128)S(1)}, f32[64,1024]{1,0:T(8,128)S(1)}) custom-call(bf16[1024,2048]{1,0:T(8,128)(2,1)} %x_ref.15, bf16[1024,2048]{1,0:T(8,128)(2,1)} %dy_ref.15, ...), custom_call_target="tpu_custom_call", output_to_operand_aliasing={{0}: (6, {}), {1}: (7, {}), {2}: (8, {}), {3}: (9, {})} | custom-call | flops 12000000000 | bytes 6291456 | tf_op jit(solution)/shard_map/inner/pallas_call | solution.py:328
  111.4 1.4 reshape.41
  112.8 1.3 reduce_sum.39
  119.4 15.6 %outer.2 = (bf16[1024,2048]{1,0:T(8,128)(2,1)}, f32[32,1024]{1,0:T(8,128)}, f32[32,1024]{1,0:T(8,128)}, bf16[1024,256]{1,0:T(8,128)(2,1)}, bf16[1024,256]{1,0:T(8,128)(2,1)}) custom-call(bf16[1024,2048]{1,0:T(8,128)(2,1)} %x_ref.15, bf16[1024,2048]{1,0:T(8,128)(2,1)} %dy_ref.15, bf16[1024,256]{1,0:T(8,128)(2,1)S(1)} %copy-done.1, ...), custom_call_target="tpu_custom_call" | custom-call | flops 2147483648 | bytes 20971520 | tf_op jit(solution)/shard_map/outer/pallas_call | solution.py:352
  135.0 15.7 %outer.3 = (bf16[1024,2048]{1,0:T(8,128)(2,1)}, f32[32,1024]{1,0:T(8,128)}, f32[32,1024]{1,0:T(8,128)}, bf16[1024,256]{1,0:T(8,128)(2,1)}, bf16[1024,256]{1,0:T(8,128)(2,1)}) custom-call(bf16[1024,2048]{1,0:T(8,128)(2,1)} %x_ref.15, bf16[1024,2048]{1,0:T(8,128)(2,1)} %dy_ref.15, ...), custom_call_target="tpu_custom_call", output_to_operand_aliasing={{0}: (18, {}), {1}: (19, {}), {2}: (20, {}), {3}: (21, {}),... | custom-call | flops 2147483648 | bytes 20971520 | tf_op jit(solution)/shard_map/outer/pallas_call | solution.py:352
  (102 shorter events, 28.2 us)
Async XLA Ops:
  10.7 15.4 %copy-start.1 = (bf16[1024,256]{1,0:T(8,128)(2,1)S(1)}, bf16[1024,256]{1,0:T(8,128)(2,1)}, u32[]{:S(2)}) copy-start(bf16[1024,256]{1,0:T(8,128)(2,1)} %k_ref.15) | copy-start | bytes 1572868
  10.7 15.4 %copy-start.3 = (bf16[1024,256]{1,0:T(8,128)(2,1)S(1)}, bf16[1024,256]{1,0:T(8,128)(2,1)}, u32[]{:S(2)}) copy-start(bf16[1024,256]{1,0:T(8,128)(2,1)} %q_ref.15) | copy-start | bytes 1572868
  23.1 14.3 %collective-permute-start = (f32[2,64,1024]{2,1,0:T(8,128)}, f32[2,64,1024]{2,1,0:T(8,128)}, u32[]{:S(2)}, u32[]{:S(2)}) collective-permute-start(f32[2,64,1024]{2,1,0:T(8,128)} %get-tuple-element.220), channel_id=1, source_target_pairs={{0,4},{4,0},{8,12},{12,8},{16,20},{20,16},{24,28},{28,24},{1,5},{5... | collective-permute-start | bytes 1572872 | tf_op jit(solution)/shard_map/ppermute | solution.py:210
  24.9 12.4 %collective-permute-start.1 = (f32[1,2048]{1,0:T(1,128)S(1)}, f32[1,2048]{1,0:T(1,128)S(1)}, u32[]{:S(2)}, u32[]{:S(2)}) collective-permute-start(f32[1,2048]{1,0:T(1,128)S(1)} %broadcast_in_dim.42), channel_id=1, source_target_pairs={{0,4},{4,0},{8,12},{12,8},{16,20},{20,16},{24,28},{28,24},{1,5},{5... | collective-permute-start | bytes 24584 | tf_op jit(solution)/shard_map/ppermute | solution.py:392
  38.0 18.6 %collective-permute-start.5 = (f32[1,2048]{1,0:T(1,128)}, f32[1,2048]{1,0:T(1,128)S(1)}, u32[]{:S(2)}, u32[]{:S(2)}) collective-permute-start(f32[1,2048]{1,0:T(1,128)} %constant_dynamic-update-slice_fusion), channel_id=1, source_target_pairs={{0,4},{4,0},{8,12},{12,8},{16,20},{20,16},{24,28},{28,24},{1,5},{5... | collective-permute-start | bytes 24584 | tf_op jit(solution)/shard_map/ppermute | solution.py:414
  40.9 15.8 %collective-permute-start.3 = (f32[64,1024]{1,0:T(8,128)S(1)}, f32[64,1024]{1,0:T(8,128)S(1)}, u32[]{:S(2)}, u32[]{:S(2)}) collective-permute-start(f32[64,1024]{1,0:T(8,128)S(1)} %get-tuple-element.216), channel_id=1, source_target_pairs={{24,16},{28,20},{25,17},{29,21},{26,18},{30,22},{27,19},{31,23}} | collective-permute-start | bytes 786440 | tf_op jit(solution)/shard_map/ppermute | solution.py:241
  41.5 15.1 %collective-permute-start.2 = (f32[64,1024]{1,0:T(8,128)S(1)}, f32[64,1024]{1,0:T(8,128)S(1)}, u32[]{:S(2)}, u32[]{:S(2)}) collective-permute-start(f32[64,1024]{1,0:T(8,128)S(1)} %get-tuple-element.217), channel_id=1, source_target_pairs={{0,8},{4,12},{1,9},{5,13},{2,10},{6,14},{3,11},{7,15}} | collective-permute-start | bytes 786440 | tf_op jit(solution)/shard_map/ppermute | solution.py:241
  43.0 13.7 %collective-permute-start.4 = (f32[2,64,1024]{2,1,0:T(8,128)S(1)}, f32[2,64,1024]{2,1,0:T(8,128)S(1)}, u32[]{:S(2)}, u32[]{:S(2)}) collective-permute-start(f32[2,64,1024]{2,1,0:T(8,128)S(1)} %get-tuple-element.214), channel_id=1, source_target_pairs={{0,4},{4,0},{8,12},{12,8},{16,20},{20,16},{24,28},{28,24},{1,5},{5... | collective-permute-start | bytes 1572872 | tf_op jit(solution)/shard_map/ppermute | solution.py:210
  57.4 16.0 %collective-permute-start.10 = (f32[1,2048]{1,0:T(1,128)S(1)}, f32[1,2048]{1,0:T(1,128)S(1)}, u32[]{:S(2)}, u32[]{:S(2)}) collective-permute-start(f32[1,2048]{1,0:T(1,128)S(1)} %add.134), channel_id=1, source_target_pairs={{0,8},{4,12},{8,0},{12,4},{16,24},{20,28},{24,16},{28,20},{1,9},{5... | collective-permute-start | bytes 24584 | tf_op jit(solution)/shard_map/ppermute | solution.py:414
  60.2 13.1 %collective-permute-start.9 = (f32[64,1024]{1,0:T(8,128)S(1)}, f32[64,1024]{1,0:T(8,128)S(1)}, u32[]{:S(2)}, u32[]{:S(2)}) collective-permute-start(f32[64,1024]{1,0:T(8,128)S(1)} %get-tuple-element.210), channel_id=1, source_target_pairs={{24,16},{28,20},{25,17},{29,21},{26,18},{30,22},{27,19},{31,23}} | collective-permute-start | bytes 786440 | tf_op jit(solution)/shard_map/ppermute | solution.py:241
  60.9 12.4 %collective-permute-start.8 = (f32[64,1024]{1,0:T(8,128)S(1)}, f32[64,1024]{1,0:T(8,128)S(1)}, u32[]{:S(2)}, u32[]{:S(2)}) collective-permute-start(f32[64,1024]{1,0:T(8,128)S(1)} %get-tuple-element.211), channel_id=1, source_target_pairs={{0,8},{4,12},{1,9},{5,13},{2,10},{6,14},{3,11},{7,15}} | collective-permute-start | bytes 786440 | tf_op jit(solution)/shard_map/ppermute | solution.py:241
  62.3 11.0 %collective-permute-start.7 = (f32[64,1024]{1,0:T(8,128)S(1)}, f32[64,1024]{1,0:T(8,128)S(1)}, u32[]{:S(2)}, u32[]{:S(2)}) collective-permute-start(f32[64,1024]{1,0:T(8,128)S(1)} %get-tuple-element.244), channel_id=1, source_target_pairs={{16,8},{20,12},{17,9},{21,13},{18,10},{22,14},{19,11},{23,15}} | collective-permute-start | bytes 786440 | tf_op jit(solution)/shard_map/ppermute | solution.py:241
  63.6 9.8 %collective-permute-start.6 = (f32[64,1024]{1,0:T(8,128)S(1)}, f32[64,1024]{1,0:T(8,128)S(1)}, u32[]{:S(2)}, u32[]{:S(2)}) collective-permute-start(f32[64,1024]{1,0:T(8,128)S(1)} %get-tuple-element.245), channel_id=1, source_target_pairs={{8,16},{12,20},{9,17},{13,21},{10,18},{14,22},{11,19},{15,23}} | collective-permute-start | bytes 786440 | tf_op jit(solution)/shard_map/ppermute | solution.py:241
  73.4 16.7 %collective-permute-start.15 = (f32[1,2048]{1,0:T(1,128)S(1)}, f32[1,2048]{1,0:T(1,128)S(1)}, u32[]{:S(2)}, u32[]{:S(2)}) collective-permute-start(f32[1,2048]{1,0:T(1,128)S(1)} %add.141), channel_id=1, source_target_pairs={{0,16},{4,20},{8,24},{12,28},{16,0},{20,4},{24,8},{28,12},{1,17},{... | collective-permute-start | bytes 24584 | tf_op jit(solution)/shard_map/ppermute | solution.py:414
  73.6 16.4 %collective-permute-start.12 = (f32[64,1024]{1,0:T(8,128)S(1)}, f32[64,1024]{1,0:T(8,128)S(1)}, u32[]{:S(2)}, u32[]{:S(2)}) collective-permute-start(f32[64,1024]{1,0:T(8,128)S(1)} %get-tuple-element.202), channel_id=1, source_target_pairs={{8,0},{12,4},{9,1},{13,5},{10,2},{14,6},{11,3},{15,7}} | collective-permute-start | bytes 786440 | tf_op jit(solution)/shard_map/ppermute | solution.py:241
  78.3 11.8 %collective-permute-start.11 = (f32[64,1024]{1,0:T(8,128)S(1)}, f32[64,1024]{1,0:T(8,128)S(1)}, u32[]{:S(2)}, u32[]{:S(2)}) collective-permute-start(f32[64,1024]{1,0:T(8,128)S(1)} %get-tuple-element.242), channel_id=1, source_target_pairs={{16,24},{20,28},{17,25},{21,29},{18,26},{22,30},{19,27},{23,31}} | collective-permute-start | bytes 786440 | tf_op jit(solution)/shard_map/ppermute | solution.py:241
  79.0 11.0 %collective-permute-start.14 = (f32[64,1024]{1,0:T(8,128)S(1)}, f32[64,1024]{1,0:T(8,128)S(1)}, u32[]{:S(2)}, u32[]{:S(2)}) collective-permute-start(f32[64,1024]{1,0:T(8,128)S(1)} %get-tuple-element.240), channel_id=1, source_target_pairs={{16,8},{20,12},{17,9},{21,13},{18,10},{22,14},{19,11},{23,15}} | collective-permute-start | bytes 786440 | tf_op jit(solution)/shard_map/ppermute | solution.py:241
  80.3 9.8 %collective-permute-start.13 = (f32[64,1024]{1,0:T(8,128)S(1)}, f32[64,1024]{1,0:T(8,128)S(1)}, u32[]{:S(2)}, u32[]{:S(2)}) collective-permute-start(f32[64,1024]{1,0:T(8,128)S(1)} %get-tuple-element.241), channel_id=1, source_target_pairs={{8,16},{12,20},{9,17},{13,21},{10,18},{14,22},{11,19},{15,23}} | collective-permute-start | bytes 786440 | tf_op jit(solution)/shard_map/ppermute | solution.py:241
  90.2 17.9 %collective-permute-start.18 = (f32[64,1024]{1,0:T(8,128)S(1)}, f32[64,1024]{1,0:T(8,128)S(1)}, u32[]{:S(2)}, u32[]{:S(2)}) collective-permute-start(f32[64,1024]{1,0:T(8,128)S(1)} %get-tuple-element.198), channel_id=1, source_target_pairs={{8,0},{12,4},{9,1},{13,5},{10,2},{14,6},{11,3},{15,7}} | collective-permute-start | bytes 786440 | tf_op jit(solution)/shard_map/ppermute | solution.py:241
  91.6 16.6 %collective-permute-start.17 = (f32[64,1024]{1,0:T(8,128)S(1)}, f32[64,1024]{1,0:T(8,128)S(1)}, u32[]{:S(2)}, u32[]{:S(2)}) collective-permute-start(f32[64,1024]{1,0:T(8,128)S(1)} %get-tuple-element.238), channel_id=1, source_target_pairs={{16,24},{20,28},{17,25},{21,29},{18,26},{22,30},{19,27},{23,31}} | collective-permute-start | bytes 786440 | tf_op jit(solution)/shard_map/ppermute | solution.py:241
  93.6 14.6 %collective-permute-start.16 = (f32[2,64,1024]{2,1,0:T(8,128)S(1)}, f32[2,64,1024]{2,1,0:T(8,128)S(1)}, u32[]{:S(2)}, u32[]{:S(2)}) collective-permute-start(f32[2,64,1024]{2,1,0:T(8,128)S(1)} %get-tuple-element.208), channel_id=1, source_target_pairs={{0,4},{4,0},{8,12},{12,8},{16,20},{20,16},{24,28},{28,24},{1,5},{5... | collective-permute-start | bytes 1572872 | tf_op jit(solution)/shard_map/ppermute | solution.py:210
  110.3 24.7 %collective-permute-start.19 = (f32[2,64,1024]{2,1,0:T(8,128)}, f32[2,64,1024]{2,1,0:T(8,128)}, u32[]{:S(2)}, u32[]{:S(2)}) collective-permute-start(f32[2,64,1024]{2,1,0:T(8,128)} %get-tuple-element.206), channel_id=1, source_target_pairs={{0,4},{4,0},{8,12},{12,8},{16,20},{20,16},{24,28},{28,24},{1,5},{5... | collective-permute-start | bytes 1572872 | tf_op jit(solution)/shard_map/ppermute | solution.py:210
  114.1 1.2 copy-start.5
  119.4 15.6 %copy-start.10 = (f32[2,64,1024]{2,1,0:T(8,128)S(1)}, f32[2,64,1024]{2,1,0:T(8,128)}, u32[]{:S(2)}) copy-start(f32[2,64,1024]{2,1,0:T(8,128)} %get-tuple-element.185.rest_0_) | copy-start | bytes 1572868
  (12 other events, 11.4 us)

commit v4 on v3

--- a/solution.py
+++ b/solution.py
@@ -10,6 +10,7 @@
 P_SIZE = 64
 N = 128
 C = 128
+LIMIT = 60 * 1024 * 1024
 INNER_MARKS = {False: (0.25, 0.4, 0.6, 0.75, 1.0), True: (0.375, 0.5, 0.625, 1.0)}
 LOG2E = 1.4426950408889634
 F32 = jnp.float32
@@ -40,7 +41,7 @@
 
 
 def params(**more):
-    return pltpu.CompilerParams(vmem_limit_bytes=48 * 1024 * 1024, **more)
+    return pltpu.CompilerParams(vmem_limit_bytes=LIMIT, **more)
 
 
 def prep_kernel(groups, per, decay_ref, step_ref, col_ref, row_ref):
@@ -69,14 +70,14 @@
 
 
 def state_kernel(per, x_ref, dy_ref, k_ref, q_ref, col_ref, tot_ref, pre_ref,
-                 h_ref, u_ref, ends_ref, skip_ref, h_s, g_s):
+                 h_ref, u_ref, ends_ref, skip_ref, h_s, g_s, skip_s):
     k = pl.program_id(0)
 
     @pl.when(k == 0)
     def _():
         h_s[...] = jnp.zeros_like(h_s)
         g_s[...] = jnp.zeros_like(g_s)
-        skip_ref[...] = jnp.zeros_like(skip_ref)
+        skip_s[...] = jnp.zeros_like(skip_s)
 
     low, _ = halves()
     keys = jnp.concatenate([k_ref[...]] * 2, axis=0)
@@ -97,12 +98,19 @@
     u_ref[0] = pull
     g_s[...] = g_s[...] + pre_ref[0] * pull
     both = x_ref[...].astype(F32) * dy_ref[...].astype(F32)
-    skip_ref[...] = skip_ref[...] + jnp.sum(both, axis=0, keepdims=True)
+    skip_s[...] = skip_s[...] + jnp.sum(both, axis=0, keepdims=True)
 
     @pl.when(k == pl.num_programs(0) - 1)
     def _():
         ends_ref[0] = h_s[...]
         ends_ref[1] = g_s[...]
+        lane = lax.broadcasted_iota(jnp.int32, (1, C), 1)
+        line = jnp.zeros((1, C), F32)
+        for j in range(per // 2):
+            pair = skip_s[:, 128 * j : 128 * (j + 1)]
+            for i, half in enumerate(halves()):
+                line = jnp.where(lane == 2 * j + i, jnp.sum(pair * half, axis=1, keepdims=True), line)
+        skip_ref[...] = line
 
 
 def inner_kernel(per, carried, x_ref, dy_ref, k_ref, q_ref, col_ref, row_ref, *rest):
@@ -221,7 +229,7 @@
     return out
 
 
-def carry_steps(ends, fades, nx, nz, x):
+def carry_steps(ends, fades, nx, nz, x, z):
     _, rows, wide = ends.shape
     got = yield exchange(ends.reshape(2, nx, rows // nx, wide), nx, x, nz)
     row_fade = fades()
@@ -234,13 +242,14 @@
     pull_sum = pulls[nx - 1]
     for i in range(nx - 2, -1, -1):
         pull_sum = row_fade[i] * pull_sum + pulls[i]
-    entering, leaving, up_send, down_send = None, None, state_sum, pull_sum
+    entering, leaving, up_send, down_send = jnp.zeros_like(state_sum), jnp.zeros_like(pull_sum), state_sum, pull_sum
     for hop in range(nz - 1):
-        up = [(hop * nx + i, (hop + 1) * nx + i) for i in range(nx)]
-        down = [((nz - 1 - hop) * nx + i, (nz - 2 - hop) * nx + i) for i in range(nx)]
-        came = yield (lax.ppermute(up_send, "ctx", up), lax.ppermute(down_send, "ctx", down))
-        entering = came[0] if hop == 0 else entering + came[0]
-        leaving = came[1] if hop == 0 else leaving + came[1]
+        down_row = nz - 1 - hop
+        pairs = [(hop * nx + i, (hop + 1) * nx + i) for i in range(nx)]
+        pairs += [(down_row * nx + i, (down_row - 1) * nx + i) for i in range(nx)]
+        came = yield lax.ppermute(jnp.where(z == hop, up_send, down_send), "ctx", pairs)
+        entering = jnp.where(z == hop + 1, came, entering)
+        leaving = jnp.where(z == down_row - 1, came, leaving)
         up_send = all_fade * entering + state_sum
         down_send = all_fade * leaving + pull_sum
     ins, outs = [entering], [leaving]
@@ -302,14 +311,14 @@
             functools.partial(state_kernel, per),
             grid=(nk,),
             in_specs=[big, big, small, small, small, tot, pre],
-            out_specs=(local, local, spec((2, N, wide), lambda k: (0, 0, 0)), spec((1, wide), lambda k: (0, 0))),
+            out_specs=(local, local, spec((2, N, wide), lambda k: (0, 0, 0)), spec((1, C), lambda k: (0, 0))),
             out_shape=(
                 jax.ShapeDtypeStruct((nk, N, wide), F32),
                 jax.ShapeDtypeStruct((nk, N, wide), F32),
                 jax.ShapeDtypeStruct((2, N, wide), F32),
-                jax.ShapeDtypeStruct((1, wide), F32),
+                jax.ShapeDtypeStruct((1, C), F32),
             ),
-            scratch_shapes=[pltpu.VMEM((N, wide), F32), pltpu.VMEM((N, wide), F32)],
+            scratch_shapes=[pltpu.VMEM((N, wide), F32), pltpu.VMEM((N, wide), F32), pltpu.VMEM((1, wide), F32)],
             compiler_params=params(),
             cost_estimate=pl.CostEstimate(
                 flops=8 * length * wide * N, bytes_accessed=12 << 20, transcendentals=0
@@ -384,7 +393,7 @@
     nx = 2 if count < 16 else 4
     nz = count // nx
     place = lax.axis_index("ctx")
-    x = place % nx
+    x, z = place % nx, place // nx
     marks = [0] + [max(1, round(nk * f)) for f in INNER_MARKS[groups > 1]]
     local, sections, arrived = {}, {}, {}
     skip, strides = None, [1 << i for i in range(count.bit_length() - 1)]
@@ -402,7 +411,7 @@
                 def faded(g=g):
                     return [f[:, g * wide : (g + 1) * wide] for f in fade_rows]
 
-                sections[g] = carry_steps(local[g][2], faded, nx, nz, x)
+                sections[g] = carry_steps(local[g][2], faded, nx, nz, x, z)
                 sent[g] = next(sections[g])
             elif g < tick <= g + nz:
                 sent[g] = sections[g].send(arrived[g])
@@ -435,7 +444,7 @@
             local[tick + 1] = made
         if not isinstance(moved_skip, tuple):
             skip = skip + moved_skip
-    grad_skip = jnp.sum(skip.reshape(heads, P_SIZE), axis=1)
+    grad_skip = skip.reshape(groups, C)[:, :per].reshape(heads)
     return (*results, grad_skip)
 
 

time: 152 us -> 141 us (0.928)
  the two profiles are of different devices: /device:TPU:8 before, /device:TPU:0 now
where the time goes in v4:
time: 141 us; the launch traced here: 140 us
  Pallas kernels  93.6 us (66%)
  starting transfers between devices  23.8 us (17%)
  other arithmetic  10.8 us (8%)
  local copies, waits for them, and re-layouts  7.57 us (5%)
  waiting for transfers between devices  2.54 us (2%)
    pallas_call x4, Pallas kernels, inner(): pl.pallas_call(functools.partial(inner_kernel, per, len(carried)), grid=(...  34.6 us
    pallas_call x2, Pallas kernels, outer(): pl.pallas_call(functools.partial(outer_kernel, per, nx, len(results)), gr...  31.9 us
    pallas_call x2, Pallas kernels, state_call(): pl.pallas_call(functools.partial(state_kernel, per), grid=(nk,), in_specs...  23.5 us
    ppermute x6, starting transfers between devices, carry_steps(): lax.ppermute(jnp.where(z == hop, up_send, down_send), 'ctx', pairs)  15.2 us
    ppermute x4, starting transfers between devices, exchange(): got.append(lax.ppermute(sent, 'ctx', pairs))  5.63 us
    select_n x6, other arithmetic, carry_steps(): jnp.where(z == hop, up_send, down_send)  4.73 us
    pallas_call x1, Pallas kernels, on_device(): pl.pallas_call(functools.partial(prep_kernel, groups, per), out_shape=(ja...  3.62 us
    ppermute x3, starting transfers between devices, on_device(): lax.ppermute(skip, 'ctx', [(i, i ^ stride) for i in range(count)])  3.01 us
  transfers between devices with their start and end apart: 14, of which 1 were waited for; matrix products, arithmetic and copies ran while one was open for 4% of the time, Pallas kernels for 45%

profile of v4, /device:TPU:0, one launch (start us, length us, event | category | flops | bytes accessed | tf_op | source)
XLA Modules:
  0.0 139.6 jit_solution(552767345417307698)
XLA Ops:
  5.1 3.6 %prep.1 = (f32[1024,256]{1,0:T(8,128)}, f32[96,1024]{1,0:T(8,128)}) custom-call(f32[32,1024]{1,0:T(8,128)} %decay_ref.1, f32[32,1024]{1,0:T(8,128)} %step_ref.5), custom_call_target="tpu_custom_call" | custom-call | tf_op jit(solution)/shard_map/prep/pallas_call | solution.py:271
  8.7 11.7 %states.2 = (f32[8,128,1024]{2,1,0:T(8,128)}, f32[8,128,1024]{2,1,0:T(8,128)}, f32[2,128,1024]{2,1,0:T(8,128)}, f32[1,128]{1,0:T(1,128)}) custom-call(bf16[1024,2048]{1,0:T(8,128)(2,1)} %x_ref.15, bf16[1024,2048]{1,0:T(8,128)(2,1)} %dy_ref.15, bf16[1024,256]{1,0:T(8,128)(2,1)} %k_ref.15, bf16[1024,256]{1,0:T(8,128)(2,1)} %q_ref.15, ...), custom_call_target="tpu_custom_call" | custom-call | flops 1073741824 | bytes 12582912 | tf_op jit(solution)/shard_map/states/pallas_call | solution.py:310
  20.4 1.3 dynamic-slice_bitcast_fusion.2
  21.7 3.0 %collective-permute-start = (f32[2,64,1024]{2,1,0:T(8,128)S(1)}, f32[2,64,1024]{2,1,0:T(8,128)S(1)}, u32[]{:S(2)}, u32[]{:S(2)}) collective-permute-start(f32[2,64,1024]{2,1,0:T(8,128)S(1)} %get-tuple-element.208), channel_id=1, source_target_pairs={{0,4},{4,0},{8,12},{12,8},{16,20},{20,16},{24,28},{28,24},{1,5},{5... | collective-permute-start | bytes 1572872 | tf_op jit(solution)/shard_map/ppermute | solution.py:218
  25.8 11.7 %states.3 = (f32[8,128,1024]{2,1,0:T(8,128)}, f32[8,128,1024]{2,1,0:T(8,128)}, f32[2,128,1024]{2,1,0:T(8,128)}, f32[1,128]{1,0:T(1,128)}) custom-call(bf16[1024,2048]{1,0:T(8,128)(2,1)} %x_ref.15, bf16[1024,2048]{1,0:T(8,128)(2,1)} %dy_ref.15, bf16[1024,256]{1,0:T(8,128)(2,1)} %k_ref.15, bf16[1024,256]{1,0:T(8,128)(2,1)} %q_ref.15, ...), custom_call_target="tpu_custom_call" | custom-call | flops 1073741824 | bytes 12582912 | tf_op jit(solution)/shard_map/states/pallas_call | solution.py:310
  38.3 2.0 %collective-permute-start.4 = (f32[1,256]{1,0:T(1,128)S(1)}, f32[1,256]{1,0:T(1,128)S(1)}, u32[]{:S(2)}, u32[]{:S(2)}) collective-permute-start(f32[1,256]{1,0:T(1,128)S(1)} %constant_dynamic-update-slice_fusion), channel_id=1, source_target_pairs={{0,4},{4,0},{8,12},{12,8},{16,20},{20,16},{24,28},{28,24},{1,5},{5... | collective-permute-start | bytes 3080 | tf_op jit(solution)/shard_map/ppermute | solution.py:423
  40.7 3.5 %collective-permute-start.2 = (f32[64,1024]{1,0:T(8,128)S(1)}, f32[64,1024]{1,0:T(8,128)S(1)}, u32[]{:S(2)}, u32[]{:S(2)}) collective-permute-start(f32[64,1024]{1,0:T(8,128)S(1)} %get-tuple-element.195), channel_id=1, source_target_pairs={{0,8},{4,12},{24,16},{28,20},{1,9},{5,13},{25,17},{29,21},{2,10},{... | collective-permute-start | bytes 786440 | tf_op jit(solution)/shard_map/ppermute | solution.py:250
  44.9 12.0 %inner.4 = (f32[1024,2048]{1,0:T(8,128)}, f32[1024,256]{1,0:T(8,128)}, f32[1024,256]{1,0:T(8,128)}, f32[64,1024]{1,0:T(8,128)}) custom-call(bf16[1024,2048]{1,0:T(8,128)(2,1)} %x_ref.15, bf16[1024,2048]{1,0:T(8,128)(2,1)} %dy_ref.15, bf16[1024,256]{1,0:T(8,128)(2,1)} %k_ref.15, bf16[1024,256]{1,0:T(8,128)(2,1)} %q_ref.15, ...), custom_call_target="tpu_custom_call" | custom-call | flops 12000000000 | bytes 6291456 | tf_op jit(solution)/shard_map/inner/pallas_call | solution.py:337
  57.8 1.4 collective-permute-start.5
  59.4 6.1 %collective-permute-start.6 = (f32[64,1024]{1,0:T(8,128)S(1)}, f32[64,1024]{1,0:T(8,128)S(1)}, u32[]{:S(2)}, u32[]{:S(2)}) collective-permute-start(f32[64,1024]{1,0:T(8,128)S(1)} %get-tuple-element.192), channel_id=1, source_target_pairs={{0,8},{4,12},{24,16},{28,20},{1,9},{5,13},{25,17},{29,21},{2,10},{... | collective-permute-start | bytes 786440 | tf_op jit(solution)/shard_map/ppermute | solution.py:250
  65.5 5.2 %inner.5 = (f32[1024,2048]{1,0:T(8,128)}, f32[1024,256]{1,0:T(8,128)}, f32[1024,256]{1,0:T(8,128)}, f32[64,1024]{1,0:T(8,128)}) custom-call(bf16[1024,2048]{1,0:T(8,128)(2,1)} %x_ref.15, bf16[1024,2048]{1,0:T(8,128)(2,1)} %dy_ref.15, bf16[1024,256]{1,0:T(8,128)(2,1)} %k_ref.15, ...), custom_call_target="tpu_custom_call", output_to_operand_aliasing={{0}: (6, {}), {1}: (7, {}), {2}: (8, {}), {3}: (9, {})} | custom-call | flops 4000000000 | bytes 2097152 | tf_op jit(solution)/shard_map/inner/pallas_call | solution.py:337
  70.7 1.9 %add_select_fusion.2 = (f32[64,1024]{1,0:T(8,128)}, f32[64,1024]{1,0:T(8,128)S(1)}, f32[64,1024]{1,0:T(8,128)}) fusion(f32[64,1024]{1,0:T(8,128)S(1)} %get-tuple-element.196, f32[64,1024]{1,0:T(8,128)S(1)} %get-tuple-element.197, f32[1024]{0:T(1024)S(1)} %bitcast.123, pred[]{:T(512)S(6)} %eq.25, f32[64,1024]{1,0:T(8,128)} %collective-permute-done.5, ...), kind=kLoop, calls=%fused_computation.42 | loop fusion | flops 589824 | bytes 1839106 | tf_op jit(solution)/shard_map/jit(_where)/select_n | solution.py:250
  73.6 1.4 collective-permute-start.9
  75.0 1.4 %collective-permute-start.8 = (f32[64,1024]{1,0:T(8,128)}, f32[64,1024]{1,0:T(8,128)}, u32[]{:S(2)}, u32[]{:S(2)}) collective-permute-start(f32[64,1024]{1,0:T(8,128)} %get-tuple-element.189), channel_id=1, source_target_pairs={{16,24},{20,28},{8,0},{12,4},{17,25},{21,29},{9,1},{13,5},{18,26},... | collective-permute-start | bytes 786440 | tf_op jit(solution)/shard_map/ppermute | solution.py:250
  76.4 5.2 %inner.6 = (f32[1024,2048]{1,0:T(8,128)}, f32[1024,256]{1,0:T(8,128)}, f32[1024,256]{1,0:T(8,128)}, f32[64,1024]{1,0:T(8,128)}) custom-call(bf16[1024,2048]{1,0:T(8,128)(2,1)} %x_ref.15, bf16[1024,2048]{1,0:T(8,128)(2,1)} %dy_ref.15, bf16[1024,256]{1,0:T(8,128)(2,1)} %k_ref.15, ...), custom_call_target="tpu_custom_call", output_to_operand_aliasing={{0}: (6, {}), {1}: (7, {}), {2}: (8, {}), {3}: (9, {})} | custom-call | flops 4000000000 | bytes 2097152 | tf_op jit(solution)/shard_map/inner/pallas_call | solution.py:337
  81.7 2.5 %collective-permute-done.8 = f32[64,1024]{1,0:T(8,128)} collective-permute-done((f32[64,1024]{1,0:T(8,128)}, f32[64,1024]{1,0:T(8,128)}, u32[]{:S(2)}, u32[]{:S(2)}) %collective-permute-start.8) | collective-permute-done | bytes 262176 | tf_op jit(solution)/shard_map/ppermute | solution.py:250
  84.2 1.8 %add_select_fusion = (f32[64,1024]{1,0:T(8,128)}, f32[64,1024]{1,0:T(8,128)S(1)}, f32[64,1024]{1,0:T(8,128)S(1)}) fusion(f32[64,1024]{1,0:T(8,128)S(1)} %get-tuple-element.193, f32[64,1024]{1,0:T(8,128)S(1)} %get-tuple-element.194, f32[1024]{0:T(1024)S(1)} %bitcast.121, pred[]{:T(512)S(6)} %eq.25, f32[64,1024]{1,0:T(8,128)} %collective-permute-done.9, ...), kind=kLoop, calls=%fused_computation.38 | loop fusion | flops 589824 | bytes 1839106 | tf_op jit(solution)/shard_map/jit(_where)/select_n | solution.py:250
  86.0 1.5 %collective-permute-start.12 = (f32[64,1024]{1,0:T(8,128)}, f32[64,1024]{1,0:T(8,128)}, u32[]{:S(2)}, u32[]{:S(2)}) collective-permute-start(f32[64,1024]{1,0:T(8,128)} %get-tuple-element.186), channel_id=1, source_target_pairs={{16,24},{20,28},{8,0},{12,4},{17,25},{21,29},{9,1},{13,5},{18,26},... | collective-permute-start | bytes 786440 | tf_op jit(solution)/shard_map/ppermute | solution.py:250
  87.4 1.1 add_bitcast_fusion.2
  89.6 1.5 %collective-permute-start.11 = (f32[2,64,1024]{2,1,0:T(8,128)S(1)}, f32[2,64,1024]{2,1,0:T(8,128)S(1)}, u32[]{:S(2)}, u32[]{:S(2)}) collective-permute-start(f32[2,64,1024]{2,1,0:T(8,128)S(1)} %get-tuple-element.200), channel_id=1, source_target_pairs={{0,4},{4,0},{8,12},{12,8},{16,20},{20,16},{24,28},{28,24},{1,5},{5... | collective-permute-start | bytes 1572872 | tf_op jit(solution)/shard_map/ppermute | solution.py:218
  91.1 12.1 %inner.7 = (f32[1024,2048]{1,0:T(8,128)}, f32[1024,256]{1,0:T(8,128)}, f32[1024,256]{1,0:T(8,128)}, f32[64,1024]{1,0:T(8,128)}) custom-call(bf16[1024,2048]{1,0:T(8,128)(2,1)} %x_ref.15, bf16[1024,2048]{1,0:T(8,128)(2,1)} %dy_ref.15, bf16[1024,256]{1,0:T(8,128)(2,1)} %k_ref.15, ...), custom_call_target="tpu_custom_call", output_to_operand_aliasing={{0}: (6, {}), {1}: (7, {}), {2}: (8, {}), {3}: (9, {})} | custom-call | flops 12000000000 | bytes 6291456 | tf_op jit(solution)/shard_map/inner/pallas_call | solution.py:337
  103.2 1.3 add_bitcast_fusion
  106.7 15.9 %outer.2 = (bf16[1024,2048]{1,0:T(8,128)(2,1)}, f32[32,1024]{1,0:T(8,128)}, f32[32,1024]{1,0:T(8,128)}, bf16[1024,256]{1,0:T(8,128)(2,1)}, bf16[1024,256]{1,0:T(8,128)(2,1)}) custom-call(bf16[1024,2048]{1,0:T(8,128)(2,1)} %x_ref.15, bf16[1024,2048]{1,0:T(8,128)(2,1)} %dy_ref.15, bf16[1024,256]{1,0:T(8,128)(2,1)} %k_ref.15, bf16[1024,256]{1,0:T(8,128)(2,1)} %q_ref.15, ...), custom_call_target="tpu_custom_call" | custom-call | flops 2147483648 | bytes 20971520 | tf_op jit(solution)/shard_map/outer/pallas_call | solution.py:361
  123.4 16.0 %outer.3 = (bf16[1024,2048]{1,0:T(8,128)(2,1)}, f32[32,1024]{1,0:T(8,128)}, f32[32,1024]{1,0:T(8,128)}, bf16[1024,256]{1,0:T(8,128)(2,1)}, bf16[1024,256]{1,0:T(8,128)(2,1)}) custom-call(bf16[1024,2048]{1,0:T(8,128)(2,1)} %x_ref.15, bf16[1024,2048]{1,0:T(8,128)(2,1)} %dy_ref.15, ...), custom_call_target="tpu_custom_call", output_to_operand_aliasing={{0}: (18, {}), {1}: (19, {}), {2}: (20, {}), {3}: (21, {}),... | custom-call | flops 2147483648 | bytes 20971520 | tf_op jit(solution)/shard_map/outer/pallas_call | solution.py:361
  (63 shorter events, 13.2 us)
Async XLA Ops:
  21.7 15.9 %collective-permute-start = (f32[2,64,1024]{2,1,0:T(8,128)S(1)}, f32[2,64,1024]{2,1,0:T(8,128)S(1)}, u32[]{:S(2)}, u32[]{:S(2)}) collective-permute-start(f32[2,64,1024]{2,1,0:T(8,128)S(1)} %get-tuple-element.208), channel_id=1, source_target_pairs={{0,4},{4,0},{8,12},{12,8},{16,20},{20,16},{24,28},{28,24},{1,5},{5... | collective-permute-start | bytes 1572872 | tf_op jit(solution)/shard_map/ppermute | solution.py:218
  25.1 12.5 %collective-permute-start.1 = (f32[1,2048]{1,0:T(1,128)S(1)}, f32[1,2048]{1,0:T(1,128)S(1)}, u32[]{:S(2)}, u32[]{:S(2)}) collective-permute-start(f32[1,2048]{1,0:T(1,128)S(1)} %broadcast_in_dim.42), channel_id=1, source_target_pairs={{0,4},{4,0},{8,12},{12,8},{16,20},{20,16},{24,28},{28,24},{1,5},{5... | collective-permute-start | bytes 24584 | tf_op jit(solution)/shard_map/ppermute | solution.py:401
  37.6 6.6 %copy-start.1 = (f32[2,128,1024]{2,1,0:T(8,128)S(1)}, f32[2,128,1024]{2,1,0:T(8,128)}, u32[]{:S(2)}) copy-start(f32[2,128,1024]{2,1,0:T(8,128)} %get-tuple-element.107) | copy-start | bytes 3145732
  38.3 18.5 %collective-permute-start.4 = (f32[1,256]{1,0:T(1,128)S(1)}, f32[1,256]{1,0:T(1,128)S(1)}, u32[]{:S(2)}, u32[]{:S(2)}) collective-permute-start(f32[1,256]{1,0:T(1,128)S(1)} %constant_dynamic-update-slice_fusion), channel_id=1, source_target_pairs={{0,4},{4,0},{8,12},{12,8},{16,20},{20,16},{24,28},{28,24},{1,5},{5... | collective-permute-start | bytes 3080 | tf_op jit(solution)/shard_map/ppermute | solution.py:423
  40.7 16.2 %collective-permute-start.2 = (f32[64,1024]{1,0:T(8,128)S(1)}, f32[64,1024]{1,0:T(8,128)S(1)}, u32[]{:S(2)}, u32[]{:S(2)}) collective-permute-start(f32[64,1024]{1,0:T(8,128)S(1)} %get-tuple-element.195), channel_id=1, source_target_pairs={{0,8},{4,12},{24,16},{28,20},{1,9},{5,13},{25,17},{29,21},{2,10},{... | collective-permute-start | bytes 786440 | tf_op jit(solution)/shard_map/ppermute | solution.py:250
  44.3 12.6 %collective-permute-start.3 = (f32[2,64,1024]{2,1,0:T(8,128)S(1)}, f32[2,64,1024]{2,1,0:T(8,128)S(1)}, u32[]{:S(2)}, u32[]{:S(2)}) collective-permute-start(f32[2,64,1024]{2,1,0:T(8,128)S(1)} %get-tuple-element.204), channel_id=1, source_target_pairs={{0,4},{4,0},{8,12},{12,8},{16,20},{20,16},{24,28},{28,24},{1,5},{5... | collective-permute-start | bytes 1572872 | tf_op jit(solution)/shard_map/ppermute | solution.py:218
  56.9 13.8 %collective-permute-start.7 = (f32[1,256]{1,0:T(1,128)S(1)}, f32[1,256]{1,0:T(1,128)S(1)}, u32[]{:S(2)}, u32[]{:S(2)}) collective-permute-start(f32[1,256]{1,0:T(1,128)S(1)} %add.111), channel_id=1, source_target_pairs={{0,8},{4,12},{8,0},{12,4},{16,24},{20,28},{24,16},{28,20},{1,9},{5... | collective-permute-start | bytes 3080 | tf_op jit(solution)/shard_map/ppermute | solution.py:423
  57.8 12.9 %collective-permute-start.5 = (f32[64,1024]{1,0:T(8,128)}, f32[64,1024]{1,0:T(8,128)}, u32[]{:S(2)}, u32[]{:S(2)}) collective-permute-start(f32[64,1024]{1,0:T(8,128)} %add_select_fusion.3), channel_id=1, source_target_pairs={{8,16},{12,20},{16,8},{20,12},{9,17},{13,21},{17,9},{21,13},{10,18... | collective-permute-start | bytes 786440 | tf_op jit(solution)/shard_map/ppermute | solution.py:250
  59.4 11.3 %collective-permute-start.6 = (f32[64,1024]{1,0:T(8,128)S(1)}, f32[64,1024]{1,0:T(8,128)S(1)}, u32[]{:S(2)}, u32[]{:S(2)}) collective-permute-start(f32[64,1024]{1,0:T(8,128)S(1)} %get-tuple-element.192), channel_id=1, source_target_pairs={{0,8},{4,12},{24,16},{28,20},{1,9},{5,13},{25,17},{29,21},{2,10},{... | collective-permute-start | bytes 786440 | tf_op jit(solution)/shard_map/ppermute | solution.py:250
  72.6 9.0 %collective-permute-start.10 = (f32[1,256]{1,0:T(1,128)S(1)}, f32[1,256]{1,0:T(1,128)S(1)}, u32[]{:S(2)}, u32[]{:S(2)}) collective-permute-start(f32[1,256]{1,0:T(1,128)S(1)} %add.116), channel_id=1, source_target_pairs={{0,16},{4,20},{8,24},{12,28},{16,0},{20,4},{24,8},{28,12},{1,17},{... | collective-permute-start | bytes 3080 | tf_op jit(solution)/shard_map/ppermute | solution.py:423
  73.6 8.0 %collective-permute-start.9 = (f32[64,1024]{1,0:T(8,128)S(1)}, f32[64,1024]{1,0:T(8,128)}, u32[]{:S(2)}, u32[]{:S(2)}) collective-permute-start(f32[64,1024]{1,0:T(8,128)S(1)} %add_select_fusion.1), channel_id=1, source_target_pairs={{8,16},{12,20},{16,8},{20,12},{9,17},{13,21},{17,9},{21,13},{10,18... | collective-permute-start | bytes 786440 | tf_op jit(solution)/shard_map/ppermute | solution.py:250
  75.0 12.4 %copy-start = (f32[64,1024]{1,0:T(8,128)S(1)}, f32[64,1024]{1,0:T(8,128)}, u32[]{:S(2)}) copy-start(f32[64,1024]{1,0:T(8,128)} %get-tuple-element.191) | copy-start | bytes 786436
  75.0 9.2 %collective-permute-start.8 = (f32[64,1024]{1,0:T(8,128)}, f32[64,1024]{1,0:T(8,128)}, u32[]{:S(2)}, u32[]{:S(2)}) collective-permute-start(f32[64,1024]{1,0:T(8,128)} %get-tuple-element.189), channel_id=1, source_target_pairs={{16,24},{20,28},{8,0},{12,4},{17,25},{21,29},{9,1},{13,5},{18,26},... | collective-permute-start | bytes 786440 | tf_op jit(solution)/shard_map/ppermute | solution.py:250
  86.0 17.2 %collective-permute-start.12 = (f32[64,1024]{1,0:T(8,128)}, f32[64,1024]{1,0:T(8,128)}, u32[]{:S(2)}, u32[]{:S(2)}) collective-permute-start(f32[64,1024]{1,0:T(8,128)} %get-tuple-element.186), channel_id=1, source_target_pairs={{16,24},{20,28},{8,0},{12,4},{17,25},{21,29},{9,1},{13,5},{18,26},... | collective-permute-start | bytes 786440 | tf_op jit(solution)/shard_map/ppermute | solution.py:250
  89.6 13.6 %collective-permute-start.11 = (f32[2,64,1024]{2,1,0:T(8,128)S(1)}, f32[2,64,1024]{2,1,0:T(8,128)S(1)}, u32[]{:S(2)}, u32[]{:S(2)}) collective-permute-start(f32[2,64,1024]{2,1,0:T(8,128)S(1)} %get-tuple-element.200), channel_id=1, source_target_pairs={{0,4},{4,0},{8,12},{12,8},{16,20},{20,16},{24,28},{28,24},{1,5},{5... | collective-permute-start | bytes 1572872 | tf_op jit(solution)/shard_map/ppermute | solution.py:218
  103.2 3.5 %copy-start.2 = (f32[2,64,1024]{2,1,0:T(8,128)}, f32[2,64,1024]{2,1,0:T(8,128)S(1)}, u32[]{:S(2)}) copy-start(f32[2,64,1024]{2,1,0:T(8,128)S(1)} %collective-permute-done.11.rest_1_) | copy-start | bytes 1572868
  105.5 17.1 %collective-permute-start.13 = (f32[2,64,1024]{2,1,0:T(8,128)S(1)}, f32[2,64,1024]{2,1,0:T(8,128)S(1)}, u32[]{:S(2)}, u32[]{:S(2)}) collective-permute-start(f32[2,64,1024]{2,1,0:T(8,128)S(1)} %get-tuple-element.198), channel_id=1, source_target_pairs={{0,4},{4,0},{8,12},{12,8},{16,20},{20,16},{24,28},{28,24},{1,5},{5... | collective-permute-start | bytes 1572872 | tf_op jit(solution)/shard_map/ppermute | solution.py:218
  122.6 0.8 copy-start.3
